TPU v7x, 256 devices: a whole 4x4x8 slice. The times are simulated.
256 devices in a mesh: section: 16 (over z, core), tensor: 8 (over y_hi, x), group: 2 (over y_lo).
Axes of the slice: x: 4, y: 4 (y_hi: 2, y_lo: 2; y = y_hi * 2 + y_lo), z: 8, core: 2. Of those that a mesh axis runs over, the one named last changes fastest.
Arguments:
- layer_deltas: bfloat16 [32, 256, 16384], P('section', 'group', 'tensor'), may hold values from -6 to 6
- tap_layers: int32 [3], replicated, may hold values from 0 to 31, as said below
- norm_gain: float32 [3, 16384], P(None, 'tensor'), may hold values from 0.1 to 1.9
- fc_weight: bfloat16 [3, 16384, 16384], P(None, 'tensor', ('section', 'group')), may hold values from -0.02734375 to 0.02734375
Outputs:
- joined: bfloat16 [256, 16384], P(None, ('section', 'group'))
Inputs may be any that keep to these rules, and one draw needn't show every extreme that they name: `tap_layers`: three layers, strictly rising: low in the first third of the 32 layers, mid in the second, high the last layer.
All inputs are finite; a program needn't handle non-finite values.
Results may differ from a plain program's by a relative error of at most 0.005.
Values may be sent and summed in bfloat16 or wider, within the bound.
No kernel may reach another device: no remote copies, remote signals or barrier semaphores. Data moves between devices by JAX's collectives and lax.ppermute only.
A program may use at most 64 MiB of HBM per device.

v0:
```python
import functools

import jax
import jax.numpy as jnp
from jax import lax
from jax.experimental import pallas as pl
from jax.experimental.pallas import tpu as pltpu
from jax.sharding import Mesh, PartitionSpec as P

D = 16384
EPS = 1e-05
ZQ, ZP, CORE, HI, X, LO = "zq", "zp", "core", "hi", "x", "lo"
Z = (ZQ, ZP)
BF, F32 = jnp.bfloat16, jnp.float32
ROWS = 16
HALF = 1024
MIB = 1 << 20

VMEM = pl.BlockSpec(memory_space=pltpu.VMEM)
SMEM = pl.BlockSpec(memory_space=pltpu.SMEM)
HBM = pl.BlockSpec(memory_space=pltpu.HBM)
ANY = pl.BlockSpec(memory_space=pl.ANY)


def call(kernel, shapes, specs, *args, flops=0, limit=24, scratch=(), alias=None):
    size = sum(a.size * a.dtype.itemsize for a in args)
    single = not isinstance(shapes, list)
    shapes = [shapes] if single else shapes
    out = pl.pallas_call(
        kernel,
        out_shape=[space(shape, kind) for shape, kind, space in shapes],
        in_specs=specs,
        out_specs=[pl.BlockSpec(memory_space=space) for _, _, space in shapes],
        scratch_shapes=list(scratch),
        input_output_aliases=alias or {},
        cost_estimate=pl.CostEstimate(flops=flops, bytes_accessed=size, transcendentals=0),
        compiler_params=pltpu.CompilerParams(vmem_limit_bytes=limit * MIB),
    )(*args)
    return out[0] if single else out


def half_of(core):
    return pl.ds(pl.multiple_of(core * HALF, HALF), HALF)


def segment(layer, tap_ref):
    return (layer > tap_ref[0]).astype(jnp.int32) + (layer > tap_ref[1]).astype(jnp.int32)


def load_kernel(tap_hbm, delta_hbm, gain_hbm, other_ref, mine_ref, tap_ref, gain_ref, three_ref, sems):
    core = lax.axis_index(CORE)
    pairs = (
        (delta_hbm.at[:, :, half_of(1 - core)], other_ref),
        (delta_hbm.at[:, :, half_of(core)], mine_ref),
        (tap_hbm, tap_ref),
        (gain_hbm, gain_ref),
    )
    copies = [pltpu.make_async_copy(a, b, sems.at[i]) for i, (a, b) in enumerate(pairs)]
    for copy in copies:
        copy.start()
    for copy in copies:
        copy.wait()
    three_ref[0] = (tap_ref[0] // 4 == tap_ref[1] // 4).astype(jnp.int32)


def pair_kernel(tap_ref, mine_ref, other_ref, ends_ref, middle_ref):
    core = lax.axis_index(CORE)
    first = (lax.axis_index(ZQ) * 2 + lax.axis_index(ZP)) * 4
    head, tail = segment(first, tap_ref), segment(first + 3, tap_ref)
    weights = []
    for side in (core, 1 - core):
        for j in range(2):
            at = segment(first + 2 * side + j, tap_ref)
            in_head = at == head
            in_tail = jnp.logical_and(at == tail, tail != head)
            between = jnp.logical_not(jnp.logical_or(in_head, in_tail))
            weights.append([jnp.where(w, 1.0, 0.0).astype(F32) for w in (in_head, in_tail, between)])
    for piece in range(8):
        rows = slice(piece * ROWS, (piece + 1) * ROWS)
        layers = [ref[j, rows].astype(F32) for ref in (mine_ref, other_ref) for j in range(2)]
        sums = []
        for part in range(3):
            terms = [layer * weight[part] for layer, weight in zip(layers, weights)]
            sums.append(((terms[0] + terms[1]) + (terms[2] + terms[3])).astype(BF))
        ends_ref[piece, 0] = sums[0]
        ends_ref[piece, 1] = sums[1]
        middle_ref[piece] = sums[2]


def tapped_kernel(tap_ref, ends_ref, middle_ref, gain_ref, out_ref):
    columns = half_of(lax.axis_index(CORE))
    between = middle_ref[0].astype(F32)
    for chip in range(1, 8):
        between = between + middle_ref[chip].astype(F32)
    for k in range(3):
        state = between if k else jnp.zeros_like(between)
        for slot in range(8):
            chip = 2 * (slot % 4) + slot // 4
            for end in range(2):
                inside = jnp.where(4 * chip + 3 * end <= tap_ref[k], 1.0, 0.0).astype(F32)
                state = state + ends_ref[slot, end].astype(F32) * inside
        out_ref[0, k] = (state * gain_ref[pl.ds(k, 1), columns]).astype(BF)


def blocks_of():
    z = 2 * lax.axis_index(ZQ) + lax.axis_index(ZP)
    mine = lax.axis_index(LO) * 8

    def block(group, step):
        chip = lax.rem(z + step, 8)
        return group + lax.rem(chip, 2) * 4 + chip // 2

    yours = 8 - mine
    early = [block(mine, step) for step in (0, 6, 2, 4)] + [block(yours, 0)]
    early += [block(mine, 7), block(mine, 5), block(yours, 7)]
    early += [block(mine, 1), block(mine, 3), block(yours, 1)]
    early += [block(yours, step) for step in (2, 6, 4)]
    return early, [block(yours, 5), block(yours, 3)]


def pack_kernel(count, *refs):
    out_ref = refs[-1]
    at = 0
    for ref in refs[:count]:
        out_ref[at : at + ref.shape[0]] = ref[...]
        at += ref.shape[0]


def ends_kernel(across_ref, left_ref, right_ref):
    left_ref[0] = across_ref[0]
    right_ref[0] = across_ref[1]


def fetch_kernel(weight_hbm, after_ref, weight_ref, sem):
    del after_ref
    copy = pltpu.make_async_copy(weight_hbm, weight_ref, sem)
    copy.start()
    copy.wait()


def join(blocks, sides, weight_ref, gain_ref, out_ref, state_ref, product_ref=None, square_ref=None):
    lane = lax.broadcasted_iota(jnp.int32, (ROWS, 128), 1) // ROWS
    squares = [[None] * 3 for _ in blocks]
    for k in range(3):
        total = None if product_ref is None else product_ref[k]
        sums = None if square_ref is None else square_ref[:, k : k + 1]
        for refs, side in sides:
            at = 0
            for ref in refs:
                rows = ref.shape[0] * ROWS
                state_ref[at : at + rows, :] = ref[:, k].reshape(rows, HALF)
                at += rows
            states = state_ref[...]
            product = jnp.dot(states, weight_ref[k, half_of(side), :], preferred_element_type=F32)
            plain = states.astype(F32) * (1.0 / gain_ref[pl.ds(k, 1), half_of(side)])
            square = jnp.sum(plain * plain, axis=1, keepdims=True)
            total = product if total is None else total + product
            sums = square if sums is None else sums + square
        total = total.astype(BF)
        for i, block in enumerate(blocks):
            rows = slice(i * ROWS, (i + 1) * ROWS)
            squares[i][k] = sums[rows]
            for column in range(4):
                at = pl.multiple_of((k * 4 + column) * 32 + lax.rem(block, 2) * ROWS, ROWS)
                out_ref[block // 2, pl.ds(at, ROWS), :] = total[rows, column * 128 : (column + 1) * 128]
    for i, block in enumerate(blocks):
        packed = out_ref[block // 2, 384:400, :].astype(F32)
        for k in range(3):
            packed = jnp.where(lane == 2 * k + lax.rem(block, 2), squares[i][k], packed)
        out_ref[block // 2, 384:400, :] = packed.astype(BF)


def early_kernel(head, middle, head_other, middle_other, weight_ref, gain_ref, out_ref, state_ref):
    core = lax.axis_index(CORE)
    out_ref[:, 384:400, :] = jnp.zeros((8, ROWS, 128), BF)
    sides = (((head, middle), core), ((head_other, middle_other), 1 - core))
    join(blocks_of()[0], sides, weight_ref, gain_ref, out_ref, state_ref)


def last_mine_kernel(last, weight_ref, gain_ref, product_ref, square_ref, state_ref):
    lane = lax.broadcasted_iota(jnp.int32, square_ref.shape, 1)
    side = half_of(lax.axis_index(CORE))
    squares = jnp.zeros(square_ref.shape, F32)
    for k in range(3):
        state_ref[...] = last[:, k].reshape(state_ref.shape)
        states = state_ref[...]
        product_ref[k] = jnp.dot(states, weight_ref[k, side, :], preferred_element_type=F32)
        plain = states.astype(F32) * (1.0 / gain_ref[pl.ds(k, 1), side])
        squares = jnp.where(lane == k, jnp.sum(plain * plain, axis=1, keepdims=True), squares)
    square_ref[...] = squares


def last_kernel(early_ref, last_other, product_ref, square_ref, weight_ref, gain_ref, out_ref, state_ref):
    del early_ref
    sides = (((last_other,), 1 - lax.axis_index(CORE)),)
    join(blocks_of()[1], sides, weight_ref, gain_ref, out_ref, state_ref, product_ref, square_ref)


def scale_kernel(parts_ref, out_ref):
    squares = parts_ref[0, 384:400, :].astype(F32)
    for piece in range(1, 8):
        squares = squares + parts_ref[piece, 384:400, :].astype(F32)
    scale = lax.rsqrt(squares / D + EPS)
    for h in range(2):
        for column in range(4):
            joined = None
            for k in range(3):
                rows = pl.ds((k * 4 + column) * 32 + h * ROWS, ROWS)
                total = parts_ref[0, rows, :].astype(F32)
                for piece in range(1, 8):
                    total = total + parts_ref[piece, rows, :].astype(F32)
                at = ROWS * (2 * k + h)
                total = total * scale[:, at : at + 1]
                joined = total if joined is None else joined + total
            joined = joined.astype(BF)
            for copy in range(8):
                out_ref[copy, h * ROWS : (h + 1) * ROWS, column * 128 : (column + 1) * 128] = joined


def swap(a, axis):
    return lax.ppermute(a, axis, [(0, 1), (1, 0)])


def along(a, step):
    return lax.ppermute(a, Z, [(i, (i + step) % 8) for i in range(8)])


def exchange(a, axes):
    return lax.all_to_all(a, axes, 0, 0, tiled=True)


def reduce_two(ends, middle):
    return exchange(ends, (ZP, ZQ)), middle


def reduce_three(ends, middle):
    parts = exchange(jnp.concatenate([ends, middle[:, None]], axis=1), (ZP, ZQ))
    return parts[:, :2], parts[:, 2]


def states(count):
    return ((count, 3, ROWS, HALF), BF, pltpu.VMEM)


def shards(layer_deltas, tap_layers, norm_gain, fc_weight):
    raw = ((2, 128, HALF), BF, pltpu.VMEM)
    sources = [pltpu.with_memory_space_constraint(a, pltpu.HBM) for a in (tap_layers, layer_deltas, norm_gain)]
    sent, own, taps, gain, three = call(
        load_kernel,
        [
            raw,
            raw,
            (tap_layers.shape, jnp.int32, pltpu.SMEM),
            (norm_gain.shape, F32, pltpu.VMEM),
            ((1,), jnp.int32, pltpu.SMEM),
        ],
        [HBM] * 3,
        *sources,
        scratch=[pltpu.SemaphoreType.DMA((4,))],
    )
    ends, middle = call(
        pair_kernel,
        [((8, 2, ROWS, HALF), BF, pltpu.VMEM), ((8, ROWS, HALF), BF, pltpu.VMEM)],
        [SMEM, VMEM, VMEM],
        taps,
        own,
        swap(sent, CORE),
    )
    ends, middle = lax.cond(three[0] != 0, reduce_three, reduce_two, ends, middle)
    piece = call(tapped_kernel, states(1), [SMEM, VMEM, VMEM, VMEM], taps, ends, middle, gain)
    far = along(piece, 4)
    below, above = along(piece, 2), along(piece, -2)
    near = swap(piece, LO)
    pack = functools.partial(pack_kernel, 3)
    across = call(pack, states(3), [VMEM] * 3, above, below, far)
    right = call(pack, states(3), [VMEM] * 3, piece, below, near)
    left = call(pack, states(3), [VMEM] * 3, piece, above, near)
    pack = functools.partial(pack_kernel, 2)
    head = call(pack, states(2), [VMEM] * 2, piece, below)
    tail = call(pack, states(2), [VMEM] * 2, above, far)
    weight = call(
        fetch_kernel,
        (fc_weight.shape, BF, pltpu.VMEM),
        [HBM, ANY],
        pltpu.with_memory_space_constraint(fc_weight, pltpu.HBM),
        across,
        scratch=[pltpu.SemaphoreType.DMA],
    )
    first = (swap(across, LO), along(right, 1), along(left, -1), swap(head, CORE), weight)
    across, from_left, from_right, head_other, weight = lax.optimization_barrier(first)
    left, right = call(ends_kernel, [states(1)] * 2, [VMEM], across)
    far_left, far_right = along(right, 1), along(left, -1)
    pack = functools.partial(pack_kernel, 5)
    middle = call(pack, states(12), [VMEM] * 5, tail, near, from_left, from_right, across)
    payload = ((8, 400, 128), BF, pltpu.VMEM)
    partial = call(
        early_kernel,
        payload,
        [VMEM] * 6,
        head,
        middle,
        head_other,
        swap(middle, CORE),
        weight,
        gain,
        flops=2 * 224 * 6144 * 512,
        scratch=[pltpu.VMEM((224, HALF), BF)],
    )
    pack = functools.partial(pack_kernel, 2)
    last = call(pack, states(2), [VMEM, VMEM, ANY], far_left, far_right, partial)
    product, square = call(
        last_mine_kernel,
        [((3, 32, 512), F32, pltpu.VMEM), ((32, 128), F32, pltpu.VMEM)],
        [VMEM] * 3,
        last,
        weight,
        gain,
        flops=32 * 6144 * 512,
        scratch=[pltpu.VMEM((32, HALF), BF)],
    )
    partial = call(
        last_kernel,
        payload,
        [VMEM] * 6,
        partial,
        swap(last, CORE),
        product,
        square,
        weight,
        gain,
        flops=32 * 6144 * 512,
        scratch=[pltpu.VMEM((32, HALF), BF)],
        alias={0: 0},
    )
    partial = exchange(partial, (X, HI))
    joined = call(scale_kernel, ((8, 32, 512), BF, pltpu.VMEM), [VMEM], partial)
    return exchange(joined, (X, HI)).reshape(256, 512)


def solution(mesh):
    fine = Mesh(mesh.devices.reshape(4, 2, 2, 2, 4, 2), (ZQ, ZP, CORE, HI, X, LO))
    section, tensor = (ZQ, ZP, CORE), (HI, X)
    in_specs = (P(section, LO, tensor), P(), P(None, tensor), P(None, tensor, (*section, LO)))
    out_specs = P(None, (*section, LO))
    return jax.shard_map(shards, mesh=fine, in_specs=in_specs, out_specs=out_specs, check_vma=False)
```

profile of v0, /device:TPU:1, one launch (start us, length us, event | category | flops | bytes accessed | tf_op | source)
XLA Modules:
  0.0 92.8 jit_solution(14354787752508867569)
XLA Ops:
  0.0 1.3 %shard_map.46 = (bf16[2,128,1024]{2,1,0:T(8,128)(2,1)S(1)}, bf16[2,128,1024]{2,1,0:T(8,128)(2,1)S(1)}, s32[3]{0:T(128)S(4)}, f32[3,2048]{1,0:T(4,128)S(1)}, s32[1]{0:T(128)S(4)}) custom-call(s32[3]{0:T(128)} %tap_hbm.1, bf16[2,128,2048]{2,1,0:T(8,128)(2,1)} %delta_hbm.1, f32[3,2048]{1,0:T(4,128)} %gain_hbm.1), custom_call_target="tpu_custom_call" | custom-call | bytes 1073164 | tf_op jit(solution)/shard_map/pallas_call | solution.py:29
  1.3 3.3 %collective-permute-start = (bf16[2,128,1024]{2,1,0:T(8,128)(2,1)S(1)}, bf16[2,128,1024]{2,1,0:T(8,128)(2,1)S(1)}, u32[]{:S(2)}, u32[]{:S(2)}) collective-permute-start(bf16[2,128,1024]{2,1,0:T(8,128)(2,1)S(1)} %get-tuple-element.38), channel_id=1, source_target_pairs={{0,16},{16,0},{1,17},{17,1},{2,18},{18,2},{3,19},{19,3},{4,20},{20... | collective-permute-start | bytes 1572872 | tf_op jit(solution)/shard_map/ppermute | solution.py:221
  4.6 1.5 %collective-permute-done.other_ref = bf16[2,128,1024]{2,1,0:T(8,128)(2,1)S(1)} collective-permute-done((bf16[2,128,1024]{2,1,0:T(8,128)(2,1)S(1)}, bf16[2,128,1024]{2,1,0:T(8,128)(2,1)S(1)}, u32[]{:S(2)}, u32[]{:S(2)}) %collective-permute-start) | collective-permute-done | bytes 524320 | tf_op jit(solution)/shard_map/ppermute | solution.py:221
  6.1 0.5 shard_map.47
  6.6 19.2 %conditional.1 = (bf16[8,2,16,1024]{3,2,1,0:T(8,128)(2,1)S(1)}, bf16[8,16,1024]{2,1,0:T(8,128)(2,1)S(1)}) conditional(s32[]{:T(128)} %bitcast.2, (bf16[8,2,16,1024]{3,2,1,0:T(8,128)(2,1)S(1)}, bf16[8,16,1024]{2,1,0:T(8,128)(2,1)S(1)}) %shard_map.47, (bf16[8,16,1024]{2,1,0:T(8,128)(2,1)S(1)}, bf16[8,2,16,1024]{3,2,1,0:T(8,128)(2,1)S(1)}) %tuple.13), branch_computations={%region_0.0_spmd, %region_1.0_spmd} | conditional | flops 393216 | bytes 4718608 | solution.py:269
  6.6 19.2 %all_to_all.18 = bf16[8,2,16,1024]{3,2,1,0:T(8,128)(2,1)S(1)} all-to-all(bf16[8,2,16,1024]{3,2,1,0:T(8,128)(2,1)S(1)} %get-tuple-element.13), channel_id=1, replica_groups=mesh['zq'=4,'zp'=2,'core'=2,'hi'=2,'x'=4,'lo'=2] {'zp','zq'}, dimensions={0} | all-to-all | bytes 1048576 | tf_op jit(solution)/shard_map/cond/branch_0_fun/all_to_all | solution.py:229
  25.8 0.4 shard_map.48.refs_0_
  26.2 1.4 %collective-permute-start.4 = (bf16[1,3,16,1024]{3,2,1,0:T(8,128)(2,1)S(1)}, bf16[1,3,16,1024]{3,2,1,0:T(8,128)(2,1)S(1)}, u32[]{:S(2)}, u32[]{:S(2)}) collective-permute-start(bf16[1,3,16,1024]{3,2,1,0:T(8,128)(2,1)S(1)} %shard_map.48.refs_0_), channel_id=1, source_target_pairs={{0,1},{1,0},{2,3},{3,2},{4,5},{5,4},{6,7},{7,6},{8,9},{9,8},{10,11... | collective-permute-start | bytes 294920 | tf_op jit(solution)/shard_map/ppermute | solution.py:221
  27.6 3.3 %collective-permute-start.2 = (bf16[1,3,16,1024]{3,2,1,0:T(8,128)(2,1)S(1)}, bf16[1,3,16,1024]{3,2,1,0:T(8,128)(2,1)S(1)}, u32[]{:S(2)}, u32[]{:S(2)}) collective-permute-start(bf16[1,3,16,1024]{3,2,1,0:T(8,128)(2,1)S(1)} %shard_map.48.refs_0_), channel_id=1, source_target_pairs={{0,192},{32,224},{64,0},{96,32},{128,64},{160,96},{192,128},{224,1... | collective-permute-start | bytes 294920 | tf_op jit(solution)/shard_map/ppermute | solution.py:225
  30.8 0.0 collective-permute-start.1
  30.8 2.9 %collective-permute-start.3 = (bf16[1,3,16,1024]{3,2,1,0:T(8,128)(2,1)S(1)}, bf16[1,3,16,1024]{3,2,1,0:T(8,128)(2,1)S(1)}, u32[]{:S(2)}, u32[]{:S(2)}) collective-permute-start(bf16[1,3,16,1024]{3,2,1,0:T(8,128)(2,1)S(1)} %shard_map.48.refs_0_), channel_id=1, source_target_pairs={{0,128},{32,160},{64,192},{96,224},{128,0},{160,32},{192,64},{224,... | collective-permute-start | bytes 294920 | tf_op jit(solution)/shard_map/ppermute | solution.py:225
  33.8 0.0 collective-permute-done.4.refs_2_.refs_1_
  33.8 0.0 collective-permute-done.2.refs_0_.refs_1_
  33.8 4.3 %collective-permute-start.7 = (bf16[3,3,16,1024]{3,2,1,0:T(8,128)(2,1)S(1)}, bf16[3,3,16,1024]{3,2,1,0:T(8,128)(2,1)S(1)}, u32[]{:S(2)}, u32[]{:S(2)}) collective-permute-start(bf16[3,3,16,1024]{3,2,1,0:T(8,128)(2,1)S(1)} %shard_map.53), channel_id=1, source_target_pairs={{0,224},{32,0},{64,32},{96,64},{128,96},{160,128},{192,160},{224,1... | collective-permute-start | bytes 884744 | tf_op jit(solution)/shard_map/ppermute | solution.py:225
  38.1 0.2 collective-permute-done.1.refs_1_
  38.3 0.1 collective-permute-start.6
  38.4 1.5 %collective-permute-done.3.refs_1_.refs_2_ = bf16[1,3,16,1024]{3,2,1,0:T(8,128)(2,1)S(1)} collective-permute-done((bf16[1,3,16,1024]{3,2,1,0:T(8,128)(2,1)S(1)}, bf16[1,3,16,1024]{3,2,1,0:T(8,128)(2,1)S(1)}, u32[]{:S(2)}, u32[]{:S(2)}) %collective-permute-start.3) | collective-permute-done | bytes 98336 | tf_op jit(solution)/shard_map/ppermute | solution.py:225
  39.9 0.3 collective-permute-start.5
  40.2 5.5 %collective-permute-start.8 = (bf16[2,3,16,1024]{3,2,1,0:T(8,128)(2,1)S(1)}, bf16[2,3,16,1024]{3,2,1,0:T(8,128)(2,1)S(1)}, u32[]{:S(2)}, u32[]{:S(2)}) collective-permute-start(bf16[2,3,16,1024]{3,2,1,0:T(8,128)(2,1)S(1)} %shard_map.49.head), channel_id=1, source_target_pairs={{0,16},{16,0},{1,17},{17,1},{2,18},{18,2},{3,19},{19,3},{4,20},{20... | collective-permute-start | bytes 589832 | tf_op jit(solution)/shard_map/ppermute | solution.py:221
  45.7 2.8 %shard_map.54.weight_ref = bf16[3,2048,512]{2,1,0:T(8,128)(2,1)S(1)} custom-call(bf16[3,2048,512]{2,1,0:T(8,128)(2,1)} %weight_hbm.1, bf16[3,3,16,1024]{3,2,1,0:T(8,128)(2,1)S(1)} %shard_map.51.after_ref), custom_call_target="tpu_custom_call" | custom-call | bytes 6586368 | tf_op jit(solution)/shard_map/pallas_call | solution.py:29
  48.5 0.0 collective-permute-done.8.head_other
  48.5 0.0 collective-permute-done.7.refs_3_
  48.5 0.0 collective-permute-done.6.refs_2_
  48.5 0.0 collective-permute-done.5.refs_4_.across_ref
  48.5 0.1 shard_map.55.middle
  48.6 3.4 %collective-permute-start.9 = (bf16[12,3,16,1024]{3,2,1,0:T(8,128)(2,1)S(1)}, bf16[12,3,16,1024]{3,2,1,0:T(8,128)(2,1)S(1)}, u32[]{:S(2)}, u32[]{:S(2)}) collective-permute-start(bf16[12,3,16,1024]{3,2,1,0:T(8,128)(2,1)S(1)} %shard_map.55.middle), channel_id=1, source_target_pairs={{0,16},{16,0},{1,17},{17,1},{2,18},{18,2},{3,19},{19,3},{4,20},{20... | collective-permute-start | bytes 3538952 | tf_op jit(solution)/shard_map/ppermute | solution.py:221
  52.0 2.8 %collective-permute-start.10 = (bf16[1,3,16,1024]{3,2,1,0:T(8,128)(2,1)S(1)}, bf16[1,3,16,1024]{3,2,1,0:T(8,128)(2,1)S(1)}, u32[]{:S(2)}, u32[]{:S(2)}) collective-permute-start(bf16[1,3,16,1024]{3,2,1,0:T(8,128)(2,1)S(1)} %get-tuple-element.49), channel_id=1, source_target_pairs={{0,32},{32,64},{64,96},{96,128},{128,160},{160,192},{192,224},{224... | collective-permute-start | bytes 294920 | tf_op jit(solution)/shard_map/ppermute | solution.py:225
  54.8 0.0 collective-permute-start.11
  54.8 0.0 collective-permute-done.9.middle_other
  54.8 2.0 %shard_map.56.refs_2_.early_ref = bf16[8,400,128]{2,1,0:T(8,128)(2,1)S(1)} custom-call(bf16[2,3,16,1024]{3,2,1,0:T(8,128)(2,1)S(1)} %shard_map.49.head, bf16[12,3,16,1024]{3,2,1,0:T(8,128)(2,1)S(1)} %shard_map.55.middle, bf16[2,3,16,1024]{3,2,1,0:T(8,128)(2,1)S(1)} %collective-permute-done.8.head_other, ...), custom_call_target="tpu_custom_call" | custom-call | flops 1409286144 | bytes 9068544 | tf_op jit(solution)/shard_map/pallas_call | solution.py:29
  56.8 0.9 collective-permute-done.10.refs_0_
  57.7 1.1 %collective-permute-done.11.refs_1_ = bf16[1,3,16,1024]{3,2,1,0:T(8,128)(2,1)S(1)} collective-permute-done((bf16[1,3,16,1024]{3,2,1,0:T(8,128)(2,1)S(1)}, bf16[1,3,16,1024]{3,2,1,0:T(8,128)(2,1)S(1)}, u32[]{:S(2)}, u32[]{:S(2)}) %collective-permute-start.11) | collective-permute-done | bytes 98336 | tf_op jit(solution)/shard_map/ppermute | solution.py:225
  58.9 1.2 %collective-permute-start.12 = (bf16[2,3,16,1024]{3,2,1,0:T(8,128)(2,1)S(1)}, bf16[2,3,16,1024]{3,2,1,0:T(8,128)(2,1)S(1)}, u32[]{:S(2)}, u32[]{:S(2)}) collective-permute-start(bf16[2,3,16,1024]{3,2,1,0:T(8,128)(2,1)S(1)} %shard_map.58.last), channel_id=1, source_target_pairs={{0,16},{16,0},{1,17},{17,1},{2,18},{18,2},{3,19},{19,3},{4,20},{20... | collective-permute-start | bytes 589832 | tf_op jit(solution)/shard_map/ppermute | solution.py:221
  60.1 0.6 shard_map.59
  60.7 0.4 collective-permute-done.12.last_other
  61.1 0.7 shard_map.60
  61.8 20.4 %all_to_all.20.parts_ref = bf16[8,400,128]{2,1,0:T(8,128)(2,1)S(1)} all-to-all(bf16[8,400,128]{2,1,0:T(8,128)(2,1)S(1)} %shard_map.60), channel_id=1, replica_groups=mesh['zq'=4,'zp'=2,'core'=2,'hi'=2,'x'=4,'lo'=2] {'x','hi'}, dimensions={0} | all-to-all | bytes 1638400 | tf_op jit(solution)/shard_map/all_to_all | solution.py:229
  82.2 0.1 shard_map.61
  82.3 9.8 %all_to_all.21 = bf16[8,32,512]{2,1,0:T(8,128)(2,1)S(1)} all-to-all(bf16[8,32,512]{2,1,0:T(8,128)(2,1)S(1)} %shard_map.61), channel_id=1, replica_groups=mesh['zq'=4,'zp'=2,'core'=2,'hi'=2,'x'=4,'lo'=2] {'x','hi'}, dimensions={0} | all-to-all | bytes 524288 | tf_op jit(solution)/shard_map/all_to_all | solution.py:229
  92.1 0.7 copy.14
  (7 shorter events, 0.1 us)
Async XLA Ops:
  1.3 4.9 %collective-permute-start = (bf16[2,128,1024]{2,1,0:T(8,128)(2,1)S(1)}, bf16[2,128,1024]{2,1,0:T(8,128)(2,1)S(1)}, u32[]{:S(2)}, u32[]{:S(2)}) collective-permute-start(bf16[2,128,1024]{2,1,0:T(8,128)(2,1)S(1)} %get-tuple-element.38), channel_id=1, source_target_pairs={{0,16},{16,0},{1,17},{17,1},{2,18},{18,2},{3,19},{19,3},{4,20},{20... | collective-permute-start | bytes 1572872 | tf_op jit(solution)/shard_map/ppermute | solution.py:221
  26.2 7.6 %collective-permute-start.4 = (bf16[1,3,16,1024]{3,2,1,0:T(8,128)(2,1)S(1)}, bf16[1,3,16,1024]{3,2,1,0:T(8,128)(2,1)S(1)}, u32[]{:S(2)}, u32[]{:S(2)}) collective-permute-start(bf16[1,3,16,1024]{3,2,1,0:T(8,128)(2,1)S(1)} %shard_map.48.refs_0_), channel_id=1, source_target_pairs={{0,1},{1,0},{2,3},{3,2},{4,5},{5,4},{6,7},{7,6},{8,9},{9,8},{10,11... | collective-permute-start | bytes 294920 | tf_op jit(solution)/shard_map/ppermute | solution.py:221
  27.6 6.2 %collective-permute-start.2 = (bf16[1,3,16,1024]{3,2,1,0:T(8,128)(2,1)S(1)}, bf16[1,3,16,1024]{3,2,1,0:T(8,128)(2,1)S(1)}, u32[]{:S(2)}, u32[]{:S(2)}) collective-permute-start(bf16[1,3,16,1024]{3,2,1,0:T(8,128)(2,1)S(1)} %shard_map.48.refs_0_), channel_id=1, source_target_pairs={{0,192},{32,224},{64,0},{96,32},{128,64},{160,96},{192,128},{224,1... | collective-permute-start | bytes 294920 | tf_op jit(solution)/shard_map/ppermute | solution.py:225
  30.8 7.4 %collective-permute-start.1 = (bf16[1,3,16,1024]{3,2,1,0:T(8,128)(2,1)S(1)}, bf16[1,3,16,1024]{3,2,1,0:T(8,128)(2,1)S(1)}, u32[]{:S(2)}, u32[]{:S(2)}) collective-permute-start(bf16[1,3,16,1024]{3,2,1,0:T(8,128)(2,1)S(1)} %shard_map.48.refs_0_), channel_id=1, source_target_pairs={{0,64},{32,96},{64,128},{96,160},{128,192},{160,224},{192,0},{224,... | collective-permute-start | bytes 294920 | tf_op jit(solution)/shard_map/ppermute | solution.py:225
  30.8 9.0 %collective-permute-start.3 = (bf16[1,3,16,1024]{3,2,1,0:T(8,128)(2,1)S(1)}, bf16[1,3,16,1024]{3,2,1,0:T(8,128)(2,1)S(1)}, u32[]{:S(2)}, u32[]{:S(2)}) collective-permute-start(bf16[1,3,16,1024]{3,2,1,0:T(8,128)(2,1)S(1)} %shard_map.48.refs_0_), channel_id=1, source_target_pairs={{0,128},{32,160},{64,192},{96,224},{128,0},{160,32},{192,64},{224,... | collective-permute-start | bytes 294920 | tf_op jit(solution)/shard_map/ppermute | solution.py:225
  33.8 14.7 %collective-permute-start.7 = (bf16[3,3,16,1024]{3,2,1,0:T(8,128)(2,1)S(1)}, bf16[3,3,16,1024]{3,2,1,0:T(8,128)(2,1)S(1)}, u32[]{:S(2)}, u32[]{:S(2)}) collective-permute-start(bf16[3,3,16,1024]{3,2,1,0:T(8,128)(2,1)S(1)} %shard_map.53), channel_id=1, source_target_pairs={{0,224},{32,0},{64,32},{96,64},{128,96},{160,128},{192,160},{224,1... | collective-permute-start | bytes 884744 | tf_op jit(solution)/shard_map/ppermute | solution.py:225
  38.3 10.2 %collective-permute-start.6 = (bf16[3,3,16,1024]{3,2,1,0:T(8,128)(2,1)S(1)}, bf16[3,3,16,1024]{3,2,1,0:T(8,128)(2,1)S(1)}, u32[]{:S(2)}, u32[]{:S(2)}) collective-permute-start(bf16[3,3,16,1024]{3,2,1,0:T(8,128)(2,1)S(1)} %shard_map.52), channel_id=1, source_target_pairs={{0,32},{32,64},{64,96},{96,128},{128,160},{160,192},{192,224},{224... | collective-permute-start | bytes 884744 | tf_op jit(solution)/shard_map/ppermute | solution.py:225
  39.9 8.6 %collective-permute-start.5 = (bf16[3,3,16,1024]{3,2,1,0:T(8,128)(2,1)S(1)}, bf16[3,3,16,1024]{3,2,1,0:T(8,128)(2,1)S(1)}, u32[]{:S(2)}, u32[]{:S(2)}) collective-permute-start(bf16[3,3,16,1024]{3,2,1,0:T(8,128)(2,1)S(1)} %shard_map.51.after_ref), channel_id=1, source_target_pairs={{0,1},{1,0},{2,3},{3,2},{4,5},{5,4},{6,7},{7,6},{8,9},{9,8},{10,11... | collective-permute-start | bytes 884744 | tf_op jit(solution)/shard_map/ppermute | solution.py:221
  40.2 8.3 %collective-permute-start.8 = (bf16[2,3,16,1024]{3,2,1,0:T(8,128)(2,1)S(1)}, bf16[2,3,16,1024]{3,2,1,0:T(8,128)(2,1)S(1)}, u32[]{:S(2)}, u32[]{:S(2)}) collective-permute-start(bf16[2,3,16,1024]{3,2,1,0:T(8,128)(2,1)S(1)} %shard_map.49.head), channel_id=1, source_target_pairs={{0,16},{16,0},{1,17},{17,1},{2,18},{18,2},{3,19},{19,3},{4,20},{20... | collective-permute-start | bytes 589832 | tf_op jit(solution)/shard_map/ppermute | solution.py:221
  48.6 6.2 %collective-permute-start.9 = (bf16[12,3,16,1024]{3,2,1,0:T(8,128)(2,1)S(1)}, bf16[12,3,16,1024]{3,2,1,0:T(8,128)(2,1)S(1)}, u32[]{:S(2)}, u32[]{:S(2)}) collective-permute-start(bf16[12,3,16,1024]{3,2,1,0:T(8,128)(2,1)S(1)} %shard_map.55.middle), channel_id=1, source_target_pairs={{0,16},{16,0},{1,17},{17,1},{2,18},{18,2},{3,19},{19,3},{4,20},{20... | collective-permute-start | bytes 3538952 | tf_op jit(solution)/shard_map/ppermute | solution.py:221
  52.0 5.7 %collective-permute-start.10 = (bf16[1,3,16,1024]{3,2,1,0:T(8,128)(2,1)S(1)}, bf16[1,3,16,1024]{3,2,1,0:T(8,128)(2,1)S(1)}, u32[]{:S(2)}, u32[]{:S(2)}) collective-permute-start(bf16[1,3,16,1024]{3,2,1,0:T(8,128)(2,1)S(1)} %get-tuple-element.49), channel_id=1, source_target_pairs={{0,32},{32,64},{64,96},{96,128},{128,160},{160,192},{192,224},{224... | collective-permute-start | bytes 294920 | tf_op jit(solution)/shard_map/ppermute | solution.py:225
  54.8 4.1 %collective-permute-start.11 = (bf16[1,3,16,1024]{3,2,1,0:T(8,128)(2,1)S(1)}, bf16[1,3,16,1024]{3,2,1,0:T(8,128)(2,1)S(1)}, u32[]{:S(2)}, u32[]{:S(2)}) collective-permute-start(bf16[1,3,16,1024]{3,2,1,0:T(8,128)(2,1)S(1)} %get-tuple-element.50), channel_id=1, source_target_pairs={{0,224},{32,0},{64,32},{96,64},{128,96},{160,128},{192,160},{224,1... | collective-permute-start | bytes 294920 | tf_op jit(solution)/shard_map/ppermute | solution.py:225
  58.9 2.3 %collective-permute-start.12 = (bf16[2,3,16,1024]{3,2,1,0:T(8,128)(2,1)S(1)}, bf16[2,3,16,1024]{3,2,1,0:T(8,128)(2,1)S(1)}, u32[]{:S(2)}, u32[]{:S(2)}) collective-permute-start(bf16[2,3,16,1024]{3,2,1,0:T(8,128)(2,1)S(1)} %shard_map.58.last), channel_id=1, source_target_pairs={{0,16},{16,0},{1,17},{17,1},{2,18},{18,2},{3,19},{19,3},{4,20},{20... | collective-permute-start | bytes 589832 | tf_op jit(solution)/shard_map/ppermute | solution.py:221
where the time goes:
time: 93 us; the launch traced here: 92.8 us
  blocking collectives  49.3 us (53%)
  starting transfers between devices  28.4 us (31%)
  Pallas kernels  8.54 us (9%)
  waiting for transfers between devices  5.71 us (6%)
    all_to_all x3, blocking collectives, exchange(): return lax.all_to_all(a, axes, 0, 0, tiled=True)  49.3 us
    ppermute x6, starting transfers between devices, swap(): return lax.ppermute(a, axis, [(0, 1), (1, 0)])  15 us
    ppermute x7, starting transfers between devices, along(): return lax.ppermute(a, Z, [(i, (i + step) % 8) for i in range(8)])  13.4 us
    pallas_call x16, Pallas kernels, call(): pl.pallas_call(kernel, out_shape=[space(shape, kind) for shape, kind, spa...  8.54 us
    ppermute x7, waiting for transfers between devices, along(): return lax.ppermute(a, Z, [(i, (i + step) % 8) for i in range(8)])  3.73 us
    ppermute x6, waiting for transfers between devices, swap(): return lax.ppermute(a, axis, [(0, 1), (1, 0)])  1.98 us
  transfers between devices with their start and end apart: 13, of which 6 were waited for; matrix products, arithmetic and copies ran while one was open for 0% of the time, Pallas kernels for 6%

commit v1 on v0

--- a/solution.py
+++ b/solution.py
@@ -47,10 +47,16 @@
     return (layer > tap_ref[0]).astype(jnp.int32) + (layer > tap_ref[1]).astype(jnp.int32)
 
 
-def load_kernel(tap_hbm, delta_hbm, gain_hbm, other_ref, mine_ref, tap_ref, gain_ref, three_ref, sems):
+def load_other_kernel(delta_hbm, other_ref, sem):
+    copy = pltpu.make_async_copy(delta_hbm.at[:, :, half_of(1 - lax.axis_index(CORE))], other_ref, sem)
+    copy.start()
+    copy.wait()
+
+
+def load_kernel(tap_hbm, delta_hbm, gain_hbm, after_ref, mine_ref, tap_ref, gain_ref, three_ref, sems):
+    del after_ref
     core = lax.axis_index(CORE)
     pairs = (
-        (delta_hbm.at[:, :, half_of(1 - core)], other_ref),
         (delta_hbm.at[:, :, half_of(core)], mine_ref),
         (tap_hbm, tap_ref),
         (gain_hbm, gain_ref),
@@ -111,11 +117,21 @@
         return group + lax.rem(chip, 2) * 4 + chip // 2
 
     yours = 8 - mine
-    early = [block(mine, step) for step in (0, 6, 2, 4)] + [block(yours, 0)]
+    early = [block(mine, step) for step in (0, 6, 2)] + [block(yours, 0)]
     early += [block(mine, 7), block(mine, 5), block(yours, 7)]
     early += [block(mine, 1), block(mine, 3), block(yours, 1)]
-    early += [block(yours, step) for step in (2, 6, 4)]
-    return early, [block(yours, 5), block(yours, 3)]
+    early += [block(yours, 2), block(yours, 6), block(mine, 4)]
+    return early, [block(yours, 4), block(yours, 5), block(yours, 3)]
+
+
+def halves_kernel(above, below, up_ref, down_ref):
+    up_ref[...] = above[:, :, :, : HALF // 2]
+    down_ref[...] = below[:, :, :, HALF // 2 :]
+
+
+def far_kernel(up, down, far_ref):
+    far_ref[:, :, :, : HALF // 2] = up[...]
+    far_ref[:, :, :, HALF // 2 :] = down[...]
 
 
 def pack_kernel(count, *refs):
@@ -170,10 +186,10 @@
         out_ref[block // 2, 384:400, :] = packed.astype(BF)
 
 
-def early_kernel(head, middle, head_other, middle_other, weight_ref, gain_ref, out_ref, state_ref):
+def early_kernel(middle, middle_other, weight_ref, gain_ref, out_ref, state_ref):
     core = lax.axis_index(CORE)
     out_ref[:, 384:400, :] = jnp.zeros((8, ROWS, 128), BF)
-    sides = (((head, middle), core), ((head_other, middle_other), 1 - core))
+    sides = (((middle,), core), ((middle_other,), 1 - core))
     join(blocks_of()[0], sides, weight_ref, gain_ref, out_ref, state_ref)
 
 
@@ -245,18 +261,19 @@
 def shards(layer_deltas, tap_layers, norm_gain, fc_weight):
     raw = ((2, 128, HALF), BF, pltpu.VMEM)
     sources = [pltpu.with_memory_space_constraint(a, pltpu.HBM) for a in (tap_layers, layer_deltas, norm_gain)]
-    sent, own, taps, gain, three = call(
+    sent = call(load_other_kernel, raw, [HBM], sources[1], scratch=[pltpu.SemaphoreType.DMA])
+    own, taps, gain, three = call(
         load_kernel,
         [
-            raw,
             raw,
             (tap_layers.shape, jnp.int32, pltpu.SMEM),
             (norm_gain.shape, F32, pltpu.VMEM),
             ((1,), jnp.int32, pltpu.SMEM),
         ],
-        [HBM] * 3,
+        [HBM] * 3 + [ANY],
         *sources,
-        scratch=[pltpu.SemaphoreType.DMA((4,))],
+        sent,
+        scratch=[pltpu.SemaphoreType.DMA((3,))],
     )
     ends, middle = call(
         pair_kernel,
@@ -268,16 +285,14 @@
     )
     ends, middle = lax.cond(three[0] != 0, reduce_three, reduce_two, ends, middle)
     piece = call(tapped_kernel, states(1), [SMEM, VMEM, VMEM, VMEM], taps, ends, middle, gain)
-    far = along(piece, 4)
     below, above = along(piece, 2), along(piece, -2)
     near = swap(piece, LO)
     pack = functools.partial(pack_kernel, 3)
-    across = call(pack, states(3), [VMEM] * 3, above, below, far)
     right = call(pack, states(3), [VMEM] * 3, piece, below, near)
     left = call(pack, states(3), [VMEM] * 3, piece, above, near)
-    pack = functools.partial(pack_kernel, 2)
-    head = call(pack, states(2), [VMEM] * 2, piece, below)
-    tail = call(pack, states(2), [VMEM] * 2, above, far)
+    across = call(functools.partial(pack_kernel, 2), states(2), [VMEM] * 2, above, below)
+    half = ((1, 3, ROWS, HALF // 2), BF, pltpu.VMEM)
+    up, down = call(halves_kernel, [half] * 2, [VMEM] * 2, above, below)
     weight = call(
         fetch_kernel,
         (fc_weight.shape, BF, pltpu.VMEM),
@@ -286,37 +301,37 @@
         across,
         scratch=[pltpu.SemaphoreType.DMA],
     )
-    first = (swap(across, LO), along(right, 1), along(left, -1), swap(head, CORE), weight)
-    across, from_left, from_right, head_other, weight = lax.optimization_barrier(first)
+    first = (swap(across, LO), along(right, 1), along(left, -1), along(up, -2), along(down, 2), weight)
+    across, from_left, from_right, up, down, weight = lax.optimization_barrier(first)
     left, right = call(ends_kernel, [states(1)] * 2, [VMEM], across)
-    far_left, far_right = along(right, 1), along(left, -1)
-    pack = functools.partial(pack_kernel, 5)
-    middle = call(pack, states(12), [VMEM] * 5, tail, near, from_left, from_right, across)
+    far = call(far_kernel, states(1), [VMEM] * 2, up, down)
+    far_left, far_right, far_across = along(right, 1), along(left, -1), swap(far, LO)
+    pack = functools.partial(pack_kernel, 8)
+    pieces = (piece, below, above, near, from_left, from_right, across, far)
+    middle = call(pack, states(13), [VMEM] * 8, *pieces)
     payload = ((8, 400, 128), BF, pltpu.VMEM)
     partial = call(
         early_kernel,
         payload,
-        [VMEM] * 6,
-        head,
+        [VMEM] * 4,
         middle,
-        head_other,
         swap(middle, CORE),
         weight,
         gain,
-        flops=2 * 224 * 6144 * 512,
-        scratch=[pltpu.VMEM((224, HALF), BF)],
-    )
-    pack = functools.partial(pack_kernel, 2)
-    last = call(pack, states(2), [VMEM, VMEM, ANY], far_left, far_right, partial)
+        flops=2 * 208 * 6144 * 512,
+        scratch=[pltpu.VMEM((208, HALF), BF)],
+    )
+    pack = functools.partial(pack_kernel, 3)
+    last = call(pack, states(3), [VMEM] * 3 + [ANY], far_across, far_left, far_right, partial)
     product, square = call(
         last_mine_kernel,
-        [((3, 32, 512), F32, pltpu.VMEM), ((32, 128), F32, pltpu.VMEM)],
+        [((3, 48, 512), F32, pltpu.VMEM), ((48, 128), F32, pltpu.VMEM)],
         [VMEM] * 3,
         last,
         weight,
         gain,
-        flops=32 * 6144 * 512,
-        scratch=[pltpu.VMEM((32, HALF), BF)],
+        flops=48 * 6144 * 512,
+        scratch=[pltpu.VMEM((48, HALF), BF)],
     )
     partial = call(
         last_kernel,
@@ -328,8 +343,8 @@
         square,
         weight,
         gain,
-        flops=32 * 6144 * 512,
-        scratch=[pltpu.VMEM((32, HALF), BF)],
+        flops=48 * 6144 * 512,
+        scratch=[pltpu.VMEM((48, HALF), BF)],
         alias={0: 0},
     )
     partial = exchange(partial, (X, HI))

time: 93 us -> 92.6 us (level)
  starting transfers between devices: 28.4 us -> 23.9 us
  waiting for transfers between devices: 5.71 us -> 8.87 us
    ppermute x7 -> x8, waiting for transfers between devices: 3.73 us -> 7.87 us  [along(): return lax.ppermute(a, Z, [(i, (i + step) % 8) for i in range(8)])]
    ppermute x7 -> x8, starting transfers between devices: 13.4 us -> 11.1 us  [along(): return lax.ppermute(a, Z, [(i, (i + step) % 8) for i in range(8)])]
    ppermute x6, starting transfers between devices: 15 us -> 12.9 us  [swap(): return lax.ppermute(a, axis, [(0, 1), (1, 0)])]
    ppermute x6, waiting for transfers between devices: 1.98 us -> 1 us  [swap(): return lax.ppermute(a, axis, [(0, 1), (1, 0)])]
    pallas_call x16 -> x17, Pallas kernels: 8.54 us -> 9.32 us  [call(): pl.pallas_call(kernel, out_shape=[space(shape, kind) for shape, kind, spa...]
  transfers between devices with their start and end apart: 13 -> 14, of which waited for: 6 -> 7; matrix products, arithmetic and copies ran while one was open for 0% -> 0% of each run, Pallas kernels for 6% -> 7%
where the time goes in v1:
time: 92.6 us; the launch traced here: 92.3 us
  blocking collectives  49.3 us (53%)
  starting transfers between devices  23.9 us (26%)
  Pallas kernels  9.32 us (10%)
  waiting for transfers between devices  8.87 us (10%)
    all_to_all x3, blocking collectives, exchange(): return lax.all_to_all(a, axes, 0, 0, tiled=True)  49.3 us
    ppermute x6, starting transfers between devices, swap(): return lax.ppermute(a, axis, [(0, 1), (1, 0)])  12.9 us
    ppermute x8, starting transfers between devices, along(): return lax.ppermute(a, Z, [(i, (i + step) % 8) for i in range(8)])  11.1 us
    pallas_call x17, Pallas kernels, call(): pl.pallas_call(kernel, out_shape=[space(shape, kind) for shape, kind, spa...  9.32 us
    ppermute x8, waiting for transfers between devices, along(): return lax.ppermute(a, Z, [(i, (i + step) % 8) for i in range(8)])  7.87 us
  transfers between devices with their start and end apart: 14, of which 7 were waited for; matrix products, arithmetic and copies ran while one was open for 0% of the time, Pallas kernels for 7%

profile of v1, /device:TPU:1, one launch (start us, length us, event | category | flops | bytes accessed | tf_op | source)
XLA Modules:
  0.0 92.3 jit_solution(387995309136962858)
XLA Ops:
  0.0 1.0 %shard_map.46.after_ref = bf16[2,128,1024]{2,1,0:T(8,128)(2,1)S(1)} custom-call(bf16[2,128,2048]{2,1,0:T(8,128)(2,1)} %delta_hbm.3), custom_call_target="tpu_custom_call" | custom-call | bytes 1048576 | tf_op jit(solution)/shard_map/pallas_call | solution.py:29
  1.1 3.3 %collective-permute-start = (bf16[2,128,1024]{2,1,0:T(8,128)(2,1)S(1)}, bf16[2,128,1024]{2,1,0:T(8,128)(2,1)S(1)}, u32[]{:S(2)}, u32[]{:S(2)}) collective-permute-start(bf16[2,128,1024]{2,1,0:T(8,128)(2,1)S(1)} %shard_map.46.after_ref), channel_id=1, source_target_pairs={{0,16},{16,0},{1,17},{17,1},{2,18},{18,2},{3,19},{19,3},{4,20},{20... | collective-permute-start | bytes 1572872 | tf_op jit(solution)/shard_map/ppermute | solution.py:237
  4.4 1.1 %shard_map.47 = (bf16[2,128,1024]{2,1,0:T(8,128)(2,1)S(1)}, s32[3]{0:T(128)S(4)}, f32[3,2048]{1,0:T(4,128)S(1)}, s32[1]{0:T(128)S(4)}) custom-call(s32[3]{0:T(128)} %tap_hbm.1, bf16[2,128,2048]{2,1,0:T(8,128)(2,1)} %delta_hbm.3, f32[3,2048]{1,0:T(4,128)} %gain_hbm.1, bf16[2,128,1024]{2,1,0:T(8,128)(2,1)S(1)} %shard_map.46.after_ref), custom_call_target="tpu_custom_call" | custom-call | bytes 1597452 | tf_op jit(solution)/shard_map/pallas_call | solution.py:29
  5.5 0.4 collective-permute-done.other_ref
  5.9 0.5 shard_map.48
  6.4 19.2 %conditional.1 = (bf16[8,2,16,1024]{3,2,1,0:T(8,128)(2,1)S(1)}, bf16[8,16,1024]{2,1,0:T(8,128)(2,1)S(1)}) conditional(s32[]{:T(128)} %bitcast.2, (bf16[8,2,16,1024]{3,2,1,0:T(8,128)(2,1)S(1)}, bf16[8,16,1024]{2,1,0:T(8,128)(2,1)S(1)}) %shard_map.48, (bf16[8,16,1024]{2,1,0:T(8,128)(2,1)S(1)}, bf16[8,2,16,1024]{3,2,1,0:T(8,128)(2,1)S(1)}) %tuple.13), branch_computations={%region_0.0_spmd, %region_1.0_spmd} | conditional | flops 393216 | bytes 4718608 | solution.py:286
  6.4 19.2 %all_to_all.18 = bf16[8,2,16,1024]{3,2,1,0:T(8,128)(2,1)S(1)} all-to-all(bf16[8,2,16,1024]{3,2,1,0:T(8,128)(2,1)S(1)} %get-tuple-element.13), channel_id=1, replica_groups=mesh['zq'=4,'zp'=2,'core'=2,'hi'=2,'x'=4,'lo'=2] {'zp','zq'}, dimensions={0} | all-to-all | bytes 1048576 | tf_op jit(solution)/shard_map/cond/branch_0_fun/all_to_all | solution.py:245
  25.6 0.4 shard_map.49.refs_0_
  26.0 1.4 %collective-permute-start.3 = (bf16[1,3,16,1024]{3,2,1,0:T(8,128)(2,1)S(1)}, bf16[1,3,16,1024]{3,2,1,0:T(8,128)(2,1)S(1)}, u32[]{:S(2)}, u32[]{:S(2)}) collective-permute-start(bf16[1,3,16,1024]{3,2,1,0:T(8,128)(2,1)S(1)} %shard_map.49.refs_0_), channel_id=1, source_target_pairs={{0,1},{1,0},{2,3},{3,2},{4,5},{5,4},{6,7},{7,6},{8,9},{9,8},{10,11... | collective-permute-start | bytes 294920 | tf_op jit(solution)/shard_map/ppermute | solution.py:237
  27.3 3.3 %collective-permute-start.2 = (bf16[1,3,16,1024]{3,2,1,0:T(8,128)(2,1)S(1)}, bf16[1,3,16,1024]{3,2,1,0:T(8,128)(2,1)S(1)}, u32[]{:S(2)}, u32[]{:S(2)}) collective-permute-start(bf16[1,3,16,1024]{3,2,1,0:T(8,128)(2,1)S(1)} %shard_map.49.refs_0_), channel_id=1, source_target_pairs={{0,192},{32,224},{64,0},{96,32},{128,64},{160,96},{192,128},{224,1... | collective-permute-start | bytes 294920 | tf_op jit(solution)/shard_map/ppermute | solution.py:241
  30.6 0.0 collective-permute-start.1
  30.6 0.0 collective-permute-done.3.refs_2_.refs_3_
  30.6 2.5 %collective-permute-done.2.refs_0_.refs_1_.above.refs_2_ = bf16[1,3,16,1024]{3,2,1,0:T(8,128)(2,1)S(1)} collective-permute-done((bf16[1,3,16,1024]{3,2,1,0:T(8,128)(2,1)S(1)}, bf16[1,3,16,1024]{3,2,1,0:T(8,128)(2,1)S(1)}, u32[]{:S(2)}, u32[]{:S(2)}) %collective-permute-start.2) | collective-permute-done | bytes 98336 | tf_op jit(solution)/shard_map/ppermute | solution.py:241
  33.1 2.2 %collective-permute-start.6 = (bf16[3,3,16,1024]{3,2,1,0:T(8,128)(2,1)S(1)}, bf16[3,3,16,1024]{3,2,1,0:T(8,128)(2,1)S(1)}, u32[]{:S(2)}, u32[]{:S(2)}) collective-permute-start(bf16[3,3,16,1024]{3,2,1,0:T(8,128)(2,1)S(1)} %shard_map.52), channel_id=1, source_target_pairs={{0,224},{32,0},{64,32},{96,64},{128,96},{160,128},{192,160},{224,1... | collective-permute-start | bytes 884744 | tf_op jit(solution)/shard_map/ppermute | solution.py:241
  35.4 1.9 %collective-permute-done.1.refs_1_.below = bf16[1,3,16,1024]{3,2,1,0:T(8,128)(2,1)S(1)} collective-permute-done((bf16[1,3,16,1024]{3,2,1,0:T(8,128)(2,1)S(1)}, bf16[1,3,16,1024]{3,2,1,0:T(8,128)(2,1)S(1)}, u32[]{:S(2)}, u32[]{:S(2)}) %collective-permute-start.1) | collective-permute-done | bytes 98336 | tf_op jit(solution)/shard_map/ppermute | solution.py:241
  37.3 0.1 collective-permute-start.5
  37.4 0.3 collective-permute-start.4
  37.7 1.7 %collective-permute-start.7 = (bf16[1,3,16,512]{3,2,1,0:T(8,128)(2,1)S(1)}, bf16[1,3,16,512]{3,2,1,0:T(8,128)(2,1)S(1)}, u32[]{:S(2)}, u32[]{:S(2)}) collective-permute-start(bf16[1,3,16,512]{3,2,1,0:T(8,128)(2,1)S(1)} %get-tuple-element.45), channel_id=1, source_target_pairs={{0,192},{32,224},{64,0},{96,32},{128,64},{160,96},{192,128},{224,1... | collective-permute-start | bytes 147464 | tf_op jit(solution)/shard_map/ppermute | solution.py:241
  39.4 0.7 collective-permute-start.8
  40.1 2.8 %shard_map.54.weight_ref = bf16[3,2048,512]{2,1,0:T(8,128)(2,1)S(1)} custom-call(bf16[3,2048,512]{2,1,0:T(8,128)(2,1)} %weight_hbm.1, bf16[2,3,16,1024]{3,2,1,0:T(8,128)(2,1)S(1)} %shard_map.50.after_ref), custom_call_target="tpu_custom_call" | custom-call | bytes 6488064 | tf_op jit(solution)/shard_map/pallas_call | solution.py:29
  42.9 0.0 collective-permute-done.7.up
  42.9 1.9 %collective-permute-done.8.down = bf16[1,3,16,512]{3,2,1,0:T(8,128)(2,1)S(1)} collective-permute-done((bf16[1,3,16,512]{3,2,1,0:T(8,128)(2,1)S(1)}, bf16[1,3,16,512]{3,2,1,0:T(8,128)(2,1)S(1)}, u32[]{:S(2)}, u32[]{:S(2)}) %collective-permute-start.8) | collective-permute-done | bytes 49184 | tf_op jit(solution)/shard_map/ppermute | solution.py:241
  44.9 0.0 collective-permute-done.4.refs_6_.across_ref
  44.9 0.0 collective-permute-done.6.refs_5_
  44.9 0.0 collective-permute-done.5.refs_4_
  44.9 0.1 shard_map.56.middle
  45.0 5.2 %collective-permute-start.9 = (bf16[13,3,16,1024]{3,2,1,0:T(8,128)(2,1)S(1)}, bf16[13,3,16,1024]{3,2,1,0:T(8,128)(2,1)S(1)}, u32[]{:S(2)}, u32[]{:S(2)}) collective-permute-start(bf16[13,3,16,1024]{3,2,1,0:T(8,128)(2,1)S(1)} %shard_map.56.middle), channel_id=1, source_target_pairs={{0,16},{16,0},{1,17},{17,1},{2,18},{18,2},{3,19},{19,3},{4,20},{20... | collective-permute-start | bytes 3833864 | tf_op jit(solution)/shard_map/ppermute | solution.py:237
  50.2 0.8 collective-permute-start.10
  51.0 3.0 %collective-permute-start.11 = (bf16[1,3,16,1024]{3,2,1,0:T(8,128)(2,1)S(1)}, bf16[1,3,16,1024]{3,2,1,0:T(8,128)(2,1)S(1)}, u32[]{:S(2)}, u32[]{:S(2)}) collective-permute-start(bf16[1,3,16,1024]{3,2,1,0:T(8,128)(2,1)S(1)} %get-tuple-element.53), channel_id=1, source_target_pairs={{0,32},{32,64},{64,96},{96,128},{128,160},{160,192},{192,224},{224... | collective-permute-start | bytes 294920 | tf_op jit(solution)/shard_map/ppermute | solution.py:241
  54.0 0.0 collective-permute-start.12
  54.0 0.0 collective-permute-done.9.middle_other
  54.0 1.9 %shard_map.57.refs_3_.early_ref = bf16[8,400,128]{2,1,0:T(8,128)(2,1)S(1)} custom-call(bf16[13,3,16,1024]{3,2,1,0:T(8,128)(2,1)S(1)} %shard_map.56.middle, bf16[13,3,16,1024]{3,2,1,0:T(8,128)(2,1)S(1)} %collective-permute-done.9.middle_other, bf16[3,2048,512]{2,1,0:T(8,128)(2,1)S(1)} %shard_map.54.weight_ref, f32[3,2048]{1,0:T(4,128)S(1)} %get-tuple-element.44.gain_ref), custom_call_target="tpu_custom_call" | custom-call | flops 1308622848 | bytes 8871936 | tf_op jit(solution)/shard_map/pallas_call | solution.py:29
  55.9 0.0 collective-permute-done.10.refs_0_
  55.9 0.4 collective-permute-done.11.refs_1_
  56.3 1.2 %collective-permute-done.12.refs_2_ = bf16[1,3,16,1024]{3,2,1,0:T(8,128)(2,1)S(1)} collective-permute-done((bf16[1,3,16,1024]{3,2,1,0:T(8,128)(2,1)S(1)}, bf16[1,3,16,1024]{3,2,1,0:T(8,128)(2,1)S(1)}, u32[]{:S(2)}, u32[]{:S(2)}) %collective-permute-start.12) | collective-permute-done | bytes 98336 | tf_op jit(solution)/shard_map/ppermute | solution.py:241
  57.5 1.9 %collective-permute-start.13 = (bf16[3,3,16,1024]{3,2,1,0:T(8,128)(2,1)S(1)}, bf16[3,3,16,1024]{3,2,1,0:T(8,128)(2,1)S(1)}, u32[]{:S(2)}, u32[]{:S(2)}) collective-permute-start(bf16[3,3,16,1024]{3,2,1,0:T(8,128)(2,1)S(1)} %shard_map.59.last), channel_id=1, source_target_pairs={{0,16},{16,0},{1,17},{17,1},{2,18},{18,2},{3,19},{19,3},{4,20},{20... | collective-permute-start | bytes 884744 | tf_op jit(solution)/shard_map/ppermute | solution.py:237
  59.4 0.6 shard_map.60
  60.0 0.6 collective-permute-done.13.last_other
  60.6 0.7 shard_map.61
  61.3 20.4 %all_to_all.20.parts_ref = bf16[8,400,128]{2,1,0:T(8,128)(2,1)S(1)} all-to-all(bf16[8,400,128]{2,1,0:T(8,128)(2,1)S(1)} %shard_map.61), channel_id=1, replica_groups=mesh['zq'=4,'zp'=2,'core'=2,'hi'=2,'x'=4,'lo'=2] {'x','hi'}, dimensions={0} | all-to-all | bytes 1638400 | tf_op jit(solution)/shard_map/all_to_all | solution.py:245
  81.7 0.1 shard_map.62
  81.8 9.8 %all_to_all.21 = bf16[8,32,512]{2,1,0:T(8,128)(2,1)S(1)} all-to-all(bf16[8,32,512]{2,1,0:T(8,128)(2,1)S(1)} %shard_map.62), channel_id=1, replica_groups=mesh['zq'=4,'zp'=2,'core'=2,'hi'=2,'x'=4,'lo'=2] {'x','hi'}, dimensions={0} | all-to-all | bytes 524288 | tf_op jit(solution)/shard_map/all_to_all | solution.py:245
  91.6 0.7 copy.14
  (7 shorter events, 0.1 us)
Async XLA Ops:
  1.1 4.9 %collective-permute-start = (bf16[2,128,1024]{2,1,0:T(8,128)(2,1)S(1)}, bf16[2,128,1024]{2,1,0:T(8,128)(2,1)S(1)}, u32[]{:S(2)}, u32[]{:S(2)}) collective-permute-start(bf16[2,128,1024]{2,1,0:T(8,128)(2,1)S(1)} %shard_map.46.after_ref), channel_id=1, source_target_pairs={{0,16},{16,0},{1,17},{17,1},{2,18},{18,2},{3,19},{19,3},{4,20},{20... | collective-permute-start | bytes 1572872 | tf_op jit(solution)/shard_map/ppermute | solution.py:237
  26.0 4.7 %collective-permute-start.3 = (bf16[1,3,16,1024]{3,2,1,0:T(8,128)(2,1)S(1)}, bf16[1,3,16,1024]{3,2,1,0:T(8,128)(2,1)S(1)}, u32[]{:S(2)}, u32[]{:S(2)}) collective-permute-start(bf16[1,3,16,1024]{3,2,1,0:T(8,128)(2,1)S(1)} %shard_map.49.refs_0_), channel_id=1, source_target_pairs={{0,1},{1,0},{2,3},{3,2},{4,5},{5,4},{6,7},{7,6},{8,9},{9,8},{10,11... | collective-permute-start | bytes 294920 | tf_op jit(solution)/shard_map/ppermute | solution.py:237
  27.3 5.8 %collective-permute-start.2 = (bf16[1,3,16,1024]{3,2,1,0:T(8,128)(2,1)S(1)}, bf16[1,3,16,1024]{3,2,1,0:T(8,128)(2,1)S(1)}, u32[]{:S(2)}, u32[]{:S(2)}) collective-permute-start(bf16[1,3,16,1024]{3,2,1,0:T(8,128)(2,1)S(1)} %shard_map.49.refs_0_), channel_id=1, source_target_pairs={{0,192},{32,224},{64,0},{96,32},{128,64},{160,96},{192,128},{224,1... | collective-permute-start | bytes 294920 | tf_op jit(solution)/shard_map/ppermute | solution.py:241
  30.6 6.6 %collective-permute-start.1 = (bf16[1,3,16,1024]{3,2,1,0:T(8,128)(2,1)S(1)}, bf16[1,3,16,1024]{3,2,1,0:T(8,128)(2,1)S(1)}, u32[]{:S(2)}, u32[]{:S(2)}) collective-permute-start(bf16[1,3,16,1024]{3,2,1,0:T(8,128)(2,1)S(1)} %shard_map.49.refs_0_), channel_id=1, source_target_pairs={{0,64},{32,96},{64,128},{96,160},{128,192},{160,224},{192,0},{224,... | collective-permute-start | bytes 294920 | tf_op jit(solution)/shard_map/ppermute | solution.py:241
  33.1 11.7 %collective-permute-start.6 = (bf16[3,3,16,1024]{3,2,1,0:T(8,128)(2,1)S(1)}, bf16[3,3,16,1024]{3,2,1,0:T(8,128)(2,1)S(1)}, u32[]{:S(2)}, u32[]{:S(2)}) collective-permute-start(bf16[3,3,16,1024]{3,2,1,0:T(8,128)(2,1)S(1)} %shard_map.52), channel_id=1, source_target_pairs={{0,224},{32,0},{64,32},{96,64},{128,96},{160,128},{192,160},{224,1... | collective-permute-start | bytes 884744 | tf_op jit(solution)/shard_map/ppermute | solution.py:241
  37.3 7.6 %collective-permute-start.5 = (bf16[3,3,16,1024]{3,2,1,0:T(8,128)(2,1)S(1)}, bf16[3,3,16,1024]{3,2,1,0:T(8,128)(2,1)S(1)}, u32[]{:S(2)}, u32[]{:S(2)}) collective-permute-start(bf16[3,3,16,1024]{3,2,1,0:T(8,128)(2,1)S(1)} %shard_map.51), channel_id=1, source_target_pairs={{0,32},{32,64},{64,96},{96,128},{128,160},{160,192},{192,224},{224... | collective-permute-start | bytes 884744 | tf_op jit(solution)/shard_map/ppermute | solution.py:241
  37.4 7.5 %collective-permute-start.4 = (bf16[2,3,16,1024]{3,2,1,0:T(8,128)(2,1)S(1)}, bf16[2,3,16,1024]{3,2,1,0:T(8,128)(2,1)S(1)}, u32[]{:S(2)}, u32[]{:S(2)}) collective-permute-start(bf16[2,3,16,1024]{3,2,1,0:T(8,128)(2,1)S(1)} %shard_map.50.after_ref), channel_id=1, source_target_pairs={{0,1},{1,0},{2,3},{3,2},{4,5},{5,4},{6,7},{7,6},{8,9},{9,8},{10,11... | collective-permute-start | bytes 589832 | tf_op jit(solution)/shard_map/ppermute | solution.py:237
  37.7 5.2 %collective-permute-start.7 = (bf16[1,3,16,512]{3,2,1,0:T(8,128)(2,1)S(1)}, bf16[1,3,16,512]{3,2,1,0:T(8,128)(2,1)S(1)}, u32[]{:S(2)}, u32[]{:S(2)}) collective-permute-start(bf16[1,3,16,512]{3,2,1,0:T(8,128)(2,1)S(1)} %get-tuple-element.45), channel_id=1, source_target_pairs={{0,192},{32,224},{64,0},{96,32},{128,64},{160,96},{192,128},{224,1... | collective-permute-start | bytes 147464 | tf_op jit(solution)/shard_map/ppermute | solution.py:241
  39.4 5.5 %collective-permute-start.8 = (bf16[1,3,16,512]{3,2,1,0:T(8,128)(2,1)S(1)}, bf16[1,3,16,512]{3,2,1,0:T(8,128)(2,1)S(1)}, u32[]{:S(2)}, u32[]{:S(2)}) collective-permute-start(bf16[1,3,16,512]{3,2,1,0:T(8,128)(2,1)S(1)} %get-tuple-element.46), channel_id=1, source_target_pairs={{0,64},{32,96},{64,128},{96,160},{128,192},{160,224},{192,0},{224,... | collective-permute-start | bytes 147464 | tf_op jit(solution)/shard_map/ppermute | solution.py:241
  45.0 9.1 %collective-permute-start.9 = (bf16[13,3,16,1024]{3,2,1,0:T(8,128)(2,1)S(1)}, bf16[13,3,16,1024]{3,2,1,0:T(8,128)(2,1)S(1)}, u32[]{:S(2)}, u32[]{:S(2)}) collective-permute-start(bf16[13,3,16,1024]{3,2,1,0:T(8,128)(2,1)S(1)} %shard_map.56.middle), channel_id=1, source_target_pairs={{0,16},{16,0},{1,17},{17,1},{2,18},{18,2},{3,19},{19,3},{4,20},{20... | collective-permute-start | bytes 3833864 | tf_op jit(solution)/shard_map/ppermute | solution.py:237
  50.2 5.7 %collective-permute-start.10 = (bf16[1,3,16,1024]{3,2,1,0:T(8,128)(2,1)S(1)}, bf16[1,3,16,1024]{3,2,1,0:T(8,128)(2,1)S(1)}, u32[]{:S(2)}, u32[]{:S(2)}) collective-permute-start(bf16[1,3,16,1024]{3,2,1,0:T(8,128)(2,1)S(1)} %shard_map.55.refs_7_), channel_id=1, source_target_pairs={{0,1},{1,0},{2,3},{3,2},{4,5},{5,4},{6,7},{7,6},{8,9},{9,8},{10,11... | collective-permute-start | bytes 294920 | tf_op jit(solution)/shard_map/ppermute | solution.py:237
  51.0 5.3 %collective-permute-start.11 = (bf16[1,3,16,1024]{3,2,1,0:T(8,128)(2,1)S(1)}, bf16[1,3,16,1024]{3,2,1,0:T(8,128)(2,1)S(1)}, u32[]{:S(2)}, u32[]{:S(2)}) collective-permute-start(bf16[1,3,16,1024]{3,2,1,0:T(8,128)(2,1)S(1)} %get-tuple-element.53), channel_id=1, source_target_pairs={{0,32},{32,64},{64,96},{96,128},{128,160},{160,192},{192,224},{224... | collective-permute-start | bytes 294920 | tf_op jit(solution)/shard_map/ppermute | solution.py:241
  54.0 3.5 %collective-permute-start.12 = (bf16[1,3,16,1024]{3,2,1,0:T(8,128)(2,1)S(1)}, bf16[1,3,16,1024]{3,2,1,0:T(8,128)(2,1)S(1)}, u32[]{:S(2)}, u32[]{:S(2)}) collective-permute-start(bf16[1,3,16,1024]{3,2,1,0:T(8,128)(2,1)S(1)} %get-tuple-element.54), channel_id=1, source_target_pairs={{0,224},{32,0},{64,32},{96,64},{128,96},{160,128},{192,160},{224,1... | collective-permute-start | bytes 294920 | tf_op jit(solution)/shard_map/ppermute | solution.py:241
  57.5 3.1 %collective-permute-start.13 = (bf16[3,3,16,1024]{3,2,1,0:T(8,128)(2,1)S(1)}, bf16[3,3,16,1024]{3,2,1,0:T(8,128)(2,1)S(1)}, u32[]{:S(2)}, u32[]{:S(2)}) collective-permute-start(bf16[3,3,16,1024]{3,2,1,0:T(8,128)(2,1)S(1)} %shard_map.59.last), channel_id=1, source_target_pairs={{0,16},{16,0},{1,17},{17,1},{2,18},{18,2},{3,19},{19,3},{4,20},{20... | collective-permute-start | bytes 884744 | tf_op jit(solution)/shard_map/ppermute | solution.py:237

commit v2 on v1

--- a/solution.py
+++ b/solution.py
@@ -193,12 +193,13 @@
     join(blocks_of()[0], sides, weight_ref, gain_ref, out_ref, state_ref)
 
 
-def last_mine_kernel(last, weight_ref, gain_ref, product_ref, square_ref, state_ref):
+def last_mine_kernel(across, last, weight_ref, gain_ref, product_ref, square_ref, state_ref):
     lane = lax.broadcasted_iota(jnp.int32, square_ref.shape, 1)
     side = half_of(lax.axis_index(CORE))
     squares = jnp.zeros(square_ref.shape, F32)
     for k in range(3):
-        state_ref[...] = last[:, k].reshape(state_ref.shape)
+        state_ref[:ROWS, :] = across[0, k]
+        state_ref[ROWS:, :] = last[:, k].reshape(2 * ROWS, HALF)
         states = state_ref[...]
         product_ref[k] = jnp.dot(states, weight_ref[k, side, :], preferred_element_type=F32)
         plain = states.astype(F32) * (1.0 / gain_ref[pl.ds(k, 1), side])
@@ -206,9 +207,9 @@
     square_ref[...] = squares
 
 
-def last_kernel(early_ref, last_other, product_ref, square_ref, weight_ref, gain_ref, out_ref, state_ref):
+def last_kernel(early_ref, across_other, last_other, product_ref, square_ref, weight_ref, gain_ref, out_ref, state_ref):
     del early_ref
-    sides = (((last_other,), 1 - lax.axis_index(CORE)),)
+    sides = (((across_other, last_other), 1 - lax.axis_index(CORE)),)
     join(blocks_of()[1], sides, weight_ref, gain_ref, out_ref, state_ref, product_ref, square_ref)
 
 
@@ -321,12 +322,13 @@
         flops=2 * 208 * 6144 * 512,
         scratch=[pltpu.VMEM((208, HALF), BF)],
     )
-    pack = functools.partial(pack_kernel, 3)
-    last = call(pack, states(3), [VMEM] * 3 + [ANY], far_across, far_left, far_right, partial)
+    pack = functools.partial(pack_kernel, 2)
+    last = call(pack, states(2), [VMEM] * 2 + [ANY], far_left, far_right, partial)
     product, square = call(
         last_mine_kernel,
         [((3, 48, 512), F32, pltpu.VMEM), ((48, 128), F32, pltpu.VMEM)],
-        [VMEM] * 3,
+        [VMEM] * 4,
+        far_across,
         last,
         weight,
         gain,
@@ -336,8 +338,9 @@
     partial = call(
         last_kernel,
         payload,
-        [VMEM] * 6,
+        [VMEM] * 7,
         partial,
+        swap(far_across, CORE),
         swap(last, CORE),
         product,
         square,

time: 92.6 us -> 92.4 us (level)
    ppermute x6 -> x7, waiting for transfers between devices: 1 us -> 2.15 us  [swap(): return lax.ppermute(a, axis, [(0, 1), (1, 0)])]
    ppermute x8, starting transfers between devices: 11.1 us -> 10 us  [along(): return lax.ppermute(a, Z, [(i, (i + step) % 8) for i in range(8)])]
    ppermute x6 -> x7, starting transfers between devices: 12.9 us -> 13.1 us  [swap(): return lax.ppermute(a, axis, [(0, 1), (1, 0)])]
  transfers between devices with their start and end apart: 14 -> 15, of which waited for: 7 -> 8; matrix products, arithmetic and copies ran while one was open for 0% -> 0% of each run, Pallas kernels for 7% -> 7%
where the time goes in v2:
time: 92.4 us; the launch traced here: 92.2 us
  blocking collectives  49.3 us (53%)
  starting transfers between devices  23.2 us (25%)
  waiting for transfers between devices  9.52 us (10%)
  Pallas kernels  9.31 us (10%)
    all_to_all x3, blocking collectives, exchange(): return lax.all_to_all(a, axes, 0, 0, tiled=True)  49.3 us
    ppermute x7, starting transfers between devices, swap(): return lax.ppermute(a, axis, [(0, 1), (1, 0)])  13.1 us
    ppermute x8, starting transfers between devices, along(): return lax.ppermute(a, Z, [(i, (i + step) % 8) for i in range(8)])  10 us
    pallas_call x17, Pallas kernels, call(): pl.pallas_call(kernel, out_shape=[space(shape, kind) for shape, kind, spa...  9.31 us
    ppermute x8, waiting for transfers between devices, along(): return lax.ppermute(a, Z, [(i, (i + step) % 8) for i in range(8)])  7.37 us
    ppermute x7, waiting for transfers between devices, swap(): return lax.ppermute(a, axis, [(0, 1), (1, 0)])  2.15 us
  transfers between devices with their start and end apart: 15, of which 8 were waited for; matrix products, arithmetic and copies ran while one was open for 0% of the time, Pallas kernels for 7%

profile of v2, /device:TPU:1, one launch (start us, length us, event | category | flops | bytes accessed | tf_op | source)
XLA Modules:
  0.0 92.2 jit_solution(1775324637899505700)
XLA Ops:
  0.0 1.0 %shard_map.46.after_ref = bf16[2,128,1024]{2,1,0:T(8,128)(2,1)S(1)} custom-call(bf16[2,128,2048]{2,1,0:T(8,128)(2,1)} %delta_hbm.3), custom_call_target="tpu_custom_call" | custom-call | bytes 1048576 | tf_op jit(solution)/shard_map/pallas_call | solution.py:29
  1.1 3.3 %collective-permute-start = (bf16[2,128,1024]{2,1,0:T(8,128)(2,1)S(1)}, bf16[2,128,1024]{2,1,0:T(8,128)(2,1)S(1)}, u32[]{:S(2)}, u32[]{:S(2)}) collective-permute-start(bf16[2,128,1024]{2,1,0:T(8,128)(2,1)S(1)} %shard_map.46.after_ref), channel_id=1, source_target_pairs={{0,16},{16,0},{1,17},{17,1},{2,18},{18,2},{3,19},{19,3},{4,20},{20... | collective-permute-start | bytes 1572872 | tf_op jit(solution)/shard_map/ppermute | solution.py:238
  4.4 1.1 %shard_map.47 = (bf16[2,128,1024]{2,1,0:T(8,128)(2,1)S(1)}, s32[3]{0:T(128)S(4)}, f32[3,2048]{1,0:T(4,128)S(1)}, s32[1]{0:T(128)S(4)}) custom-call(s32[3]{0:T(128)} %tap_hbm.1, bf16[2,128,2048]{2,1,0:T(8,128)(2,1)} %delta_hbm.3, f32[3,2048]{1,0:T(4,128)} %gain_hbm.1, bf16[2,128,1024]{2,1,0:T(8,128)(2,1)S(1)} %shard_map.46.after_ref), custom_call_target="tpu_custom_call" | custom-call | bytes 1597452 | tf_op jit(solution)/shard_map/pallas_call | solution.py:29
  5.5 0.4 collective-permute-done.other_ref
  5.9 0.5 shard_map.48
  6.4 19.2 %conditional.1 = (bf16[8,2,16,1024]{3,2,1,0:T(8,128)(2,1)S(1)}, bf16[8,16,1024]{2,1,0:T(8,128)(2,1)S(1)}) conditional(s32[]{:T(128)} %bitcast.2, (bf16[8,2,16,1024]{3,2,1,0:T(8,128)(2,1)S(1)}, bf16[8,16,1024]{2,1,0:T(8,128)(2,1)S(1)}) %shard_map.48, (bf16[8,16,1024]{2,1,0:T(8,128)(2,1)S(1)}, bf16[8,2,16,1024]{3,2,1,0:T(8,128)(2,1)S(1)}) %tuple.13), branch_computations={%region_0.0_spmd, %region_1.0_spmd} | conditional | flops 393216 | bytes 4718608 | solution.py:287
  6.4 19.2 %all_to_all.18 = bf16[8,2,16,1024]{3,2,1,0:T(8,128)(2,1)S(1)} all-to-all(bf16[8,2,16,1024]{3,2,1,0:T(8,128)(2,1)S(1)} %get-tuple-element.13), channel_id=1, replica_groups=mesh['zq'=4,'zp'=2,'core'=2,'hi'=2,'x'=4,'lo'=2] {'zp','zq'}, dimensions={0} | all-to-all | bytes 1048576 | tf_op jit(solution)/shard_map/cond/branch_0_fun/all_to_all | solution.py:246
  25.6 0.4 shard_map.49.refs_0_
  26.0 3.4 %collective-permute-start.2 = (bf16[1,3,16,1024]{3,2,1,0:T(8,128)(2,1)S(1)}, bf16[1,3,16,1024]{3,2,1,0:T(8,128)(2,1)S(1)}, u32[]{:S(2)}, u32[]{:S(2)}) collective-permute-start(bf16[1,3,16,1024]{3,2,1,0:T(8,128)(2,1)S(1)} %shard_map.49.refs_0_), channel_id=1, source_target_pairs={{0,192},{32,224},{64,0},{96,32},{128,64},{160,96},{192,128},{224,1... | collective-permute-start | bytes 294920 | tf_op jit(solution)/shard_map/ppermute | solution.py:242
  29.3 1.3 %collective-permute-start.3 = (bf16[1,3,16,1024]{3,2,1,0:T(8,128)(2,1)S(1)}, bf16[1,3,16,1024]{3,2,1,0:T(8,128)(2,1)S(1)}, u32[]{:S(2)}, u32[]{:S(2)}) collective-permute-start(bf16[1,3,16,1024]{3,2,1,0:T(8,128)(2,1)S(1)} %shard_map.49.refs_0_), channel_id=1, source_target_pairs={{0,1},{1,0},{2,3},{3,2},{4,5},{5,4},{6,7},{7,6},{8,9},{9,8},{10,11... | collective-permute-start | bytes 294920 | tf_op jit(solution)/shard_map/ppermute | solution.py:238
  30.6 0.0 collective-permute-start.1
  30.6 1.3 %collective-permute-done.2.refs_0_.refs_1_.above.refs_2_ = bf16[1,3,16,1024]{3,2,1,0:T(8,128)(2,1)S(1)} collective-permute-done((bf16[1,3,16,1024]{3,2,1,0:T(8,128)(2,1)S(1)}, bf16[1,3,16,1024]{3,2,1,0:T(8,128)(2,1)S(1)}, u32[]{:S(2)}, u32[]{:S(2)}) %collective-permute-start.2) | collective-permute-done | bytes 98336 | tf_op jit(solution)/shard_map/ppermute | solution.py:242
  31.9 1.2 %collective-permute-done.3.refs_2_.refs_3_ = bf16[1,3,16,1024]{3,2,1,0:T(8,128)(2,1)S(1)} collective-permute-done((bf16[1,3,16,1024]{3,2,1,0:T(8,128)(2,1)S(1)}, bf16[1,3,16,1024]{3,2,1,0:T(8,128)(2,1)S(1)}, u32[]{:S(2)}, u32[]{:S(2)}) %collective-permute-start.3) | collective-permute-done | bytes 98336 | tf_op jit(solution)/shard_map/ppermute | solution.py:238
  33.1 1.5 %collective-permute-start.6 = (bf16[3,3,16,1024]{3,2,1,0:T(8,128)(2,1)S(1)}, bf16[3,3,16,1024]{3,2,1,0:T(8,128)(2,1)S(1)}, u32[]{:S(2)}, u32[]{:S(2)}) collective-permute-start(bf16[3,3,16,1024]{3,2,1,0:T(8,128)(2,1)S(1)} %shard_map.52), channel_id=1, source_target_pairs={{0,224},{32,0},{64,32},{96,64},{128,96},{160,128},{192,160},{224,1... | collective-permute-start | bytes 884744 | tf_op jit(solution)/shard_map/ppermute | solution.py:242
  34.6 2.7 %collective-permute-done.1.refs_1_.below = bf16[1,3,16,1024]{3,2,1,0:T(8,128)(2,1)S(1)} collective-permute-done((bf16[1,3,16,1024]{3,2,1,0:T(8,128)(2,1)S(1)}, bf16[1,3,16,1024]{3,2,1,0:T(8,128)(2,1)S(1)}, u32[]{:S(2)}, u32[]{:S(2)}) %collective-permute-start.1) | collective-permute-done | bytes 98336 | tf_op jit(solution)/shard_map/ppermute | solution.py:242
  37.3 0.1 collective-permute-start.5
  37.4 0.3 collective-permute-start.4
  37.6 1.5 %collective-permute-start.7 = (bf16[1,3,16,512]{3,2,1,0:T(8,128)(2,1)S(1)}, bf16[1,3,16,512]{3,2,1,0:T(8,128)(2,1)S(1)}, u32[]{:S(2)}, u32[]{:S(2)}) collective-permute-start(bf16[1,3,16,512]{3,2,1,0:T(8,128)(2,1)S(1)} %get-tuple-element.45), channel_id=1, source_target_pairs={{0,192},{32,224},{64,0},{96,32},{128,64},{160,96},{192,128},{224,1... | collective-permute-start | bytes 147464 | tf_op jit(solution)/shard_map/ppermute | solution.py:242
  39.2 0.9 collective-permute-start.8
  40.1 2.8 %shard_map.54.weight_ref = bf16[3,2048,512]{2,1,0:T(8,128)(2,1)S(1)} custom-call(bf16[3,2048,512]{2,1,0:T(8,128)(2,1)} %weight_hbm.1, bf16[2,3,16,1024]{3,2,1,0:T(8,128)(2,1)S(1)} %shard_map.50.after_ref), custom_call_target="tpu_custom_call" | custom-call | bytes 6488064 | tf_op jit(solution)/shard_map/pallas_call | solution.py:29
  42.9 0.0 collective-permute-done.7.up
  42.9 1.8 %collective-permute-done.8.down = bf16[1,3,16,512]{3,2,1,0:T(8,128)(2,1)S(1)} collective-permute-done((bf16[1,3,16,512]{3,2,1,0:T(8,128)(2,1)S(1)}, bf16[1,3,16,512]{3,2,1,0:T(8,128)(2,1)S(1)}, u32[]{:S(2)}, u32[]{:S(2)}) %collective-permute-start.8) | collective-permute-done | bytes 49184 | tf_op jit(solution)/shard_map/ppermute | solution.py:242
  44.7 0.0 collective-permute-done.4.refs_6_.across_ref
  44.7 0.0 collective-permute-done.6.refs_5_
  44.7 0.0 collective-permute-done.5.refs_4_
  44.7 0.1 shard_map.56.middle
  44.8 5.2 %collective-permute-start.9 = (bf16[13,3,16,1024]{3,2,1,0:T(8,128)(2,1)S(1)}, bf16[13,3,16,1024]{3,2,1,0:T(8,128)(2,1)S(1)}, u32[]{:S(2)}, u32[]{:S(2)}) collective-permute-start(bf16[13,3,16,1024]{3,2,1,0:T(8,128)(2,1)S(1)} %shard_map.56.middle), channel_id=1, source_target_pairs={{0,16},{16,0},{1,17},{17,1},{2,18},{18,2},{3,19},{19,3},{4,20},{20... | collective-permute-start | bytes 3833864 | tf_op jit(solution)/shard_map/ppermute | solution.py:238
  50.1 1.4 %collective-permute-start.10 = (bf16[1,3,16,1024]{3,2,1,0:T(8,128)(2,1)S(1)}, bf16[1,3,16,1024]{3,2,1,0:T(8,128)(2,1)S(1)}, u32[]{:S(2)}, u32[]{:S(2)}) collective-permute-start(bf16[1,3,16,1024]{3,2,1,0:T(8,128)(2,1)S(1)} %shard_map.55.refs_7_), channel_id=1, source_target_pairs={{0,1},{1,0},{2,3},{3,2},{4,5},{5,4},{6,7},{7,6},{8,9},{9,8},{10,11... | collective-permute-start | bytes 294920 | tf_op jit(solution)/shard_map/ppermute | solution.py:238
  51.5 2.4 %collective-permute-start.12 = (bf16[1,3,16,1024]{3,2,1,0:T(8,128)(2,1)S(1)}, bf16[1,3,16,1024]{3,2,1,0:T(8,128)(2,1)S(1)}, u32[]{:S(2)}, u32[]{:S(2)}) collective-permute-start(bf16[1,3,16,1024]{3,2,1,0:T(8,128)(2,1)S(1)} %get-tuple-element.53), channel_id=1, source_target_pairs={{0,32},{32,64},{64,96},{96,128},{128,160},{160,192},{192,224},{224... | collective-permute-start | bytes 294920 | tf_op jit(solution)/shard_map/ppermute | solution.py:242
  53.9 0.3 collective-permute-start.13
  54.1 0.0 collective-permute-done.9.middle_other
  54.1 1.9 %shard_map.57.refs_2_.early_ref = bf16[8,400,128]{2,1,0:T(8,128)(2,1)S(1)} custom-call(bf16[13,3,16,1024]{3,2,1,0:T(8,128)(2,1)S(1)} %shard_map.56.middle, bf16[13,3,16,1024]{3,2,1,0:T(8,128)(2,1)S(1)} %collective-permute-done.9.middle_other, bf16[3,2048,512]{2,1,0:T(8,128)(2,1)S(1)} %shard_map.54.weight_ref, f32[3,2048]{1,0:T(4,128)S(1)} %get-tuple-element.44.gain_ref), custom_call_target="tpu_custom_call" | custom-call | flops 1308622848 | bytes 8871936 | tf_op jit(solution)/shard_map/pallas_call | solution.py:29
  56.0 0.7 collective-permute-done.12.refs_0_
  56.8 0.9 collective-permute-done.13.refs_1_
  57.6 1.5 %collective-permute-start.14 = (bf16[2,3,16,1024]{3,2,1,0:T(8,128)(2,1)S(1)}, bf16[2,3,16,1024]{3,2,1,0:T(8,128)(2,1)S(1)}, u32[]{:S(2)}, u32[]{:S(2)}) collective-permute-start(bf16[2,3,16,1024]{3,2,1,0:T(8,128)(2,1)S(1)} %shard_map.59.last), channel_id=1, source_target_pairs={{0,16},{16,0},{1,17},{17,1},{2,18},{18,2},{3,19},{19,3},{4,20},{20... | collective-permute-start | bytes 589832 | tf_op jit(solution)/shard_map/ppermute | solution.py:238
  59.2 0.0 collective-permute-done.10.across
  59.2 0.1 collective-permute-start.11
  59.3 0.6 shard_map.60
  59.9 0.5 collective-permute-done.11.across_other
  60.5 0.0 collective-permute-done.14.last_other
  60.5 0.7 shard_map.61
  61.2 20.3 %all_to_all.20.parts_ref = bf16[8,400,128]{2,1,0:T(8,128)(2,1)S(1)} all-to-all(bf16[8,400,128]{2,1,0:T(8,128)(2,1)S(1)} %shard_map.61), channel_id=1, replica_groups=mesh['zq'=4,'zp'=2,'core'=2,'hi'=2,'x'=4,'lo'=2] {'x','hi'}, dimensions={0} | all-to-all | bytes 1638400 | tf_op jit(solution)/shard_map/all_to_all | solution.py:246
  81.5 0.1 shard_map.62
  81.6 9.8 %all_to_all.21 = bf16[8,32,512]{2,1,0:T(8,128)(2,1)S(1)} all-to-all(bf16[8,32,512]{2,1,0:T(8,128)(2,1)S(1)} %shard_map.62), channel_id=1, replica_groups=mesh['zq'=4,'zp'=2,'core'=2,'hi'=2,'x'=4,'lo'=2] {'x','hi'}, dimensions={0} | all-to-all | bytes 524288 | tf_op jit(solution)/shard_map/all_to_all | solution.py:246
  91.5 0.7 copy.14
  (7 shorter events, 0.1 us)
Async XLA Ops:
  1.1 4.9 %collective-permute-start = (bf16[2,128,1024]{2,1,0:T(8,128)(2,1)S(1)}, bf16[2,128,1024]{2,1,0:T(8,128)(2,1)S(1)}, u32[]{:S(2)}, u32[]{:S(2)}) collective-permute-start(bf16[2,128,1024]{2,1,0:T(8,128)(2,1)S(1)} %shard_map.46.after_ref), channel_id=1, source_target_pairs={{0,16},{16,0},{1,17},{17,1},{2,18},{18,2},{3,19},{19,3},{4,20},{20... | collective-permute-start | bytes 1572872 | tf_op jit(solution)/shard_map/ppermute | solution.py:238
  26.0 6.0 %collective-permute-start.2 = (bf16[1,3,16,1024]{3,2,1,0:T(8,128)(2,1)S(1)}, bf16[1,3,16,1024]{3,2,1,0:T(8,128)(2,1)S(1)}, u32[]{:S(2)}, u32[]{:S(2)}) collective-permute-start(bf16[1,3,16,1024]{3,2,1,0:T(8,128)(2,1)S(1)} %shard_map.49.refs_0_), channel_id=1, source_target_pairs={{0,192},{32,224},{64,0},{96,32},{128,64},{160,96},{192,128},{224,1... | collective-permute-start | bytes 294920 | tf_op jit(solution)/shard_map/ppermute | solution.py:242
  29.3 3.8 %collective-permute-start.3 = (bf16[1,3,16,1024]{3,2,1,0:T(8,128)(2,1)S(1)}, bf16[1,3,16,1024]{3,2,1,0:T(8,128)(2,1)S(1)}, u32[]{:S(2)}, u32[]{:S(2)}) collective-permute-start(bf16[1,3,16,1024]{3,2,1,0:T(8,128)(2,1)S(1)} %shard_map.49.refs_0_), channel_id=1, source_target_pairs={{0,1},{1,0},{2,3},{3,2},{4,5},{5,4},{6,7},{7,6},{8,9},{9,8},{10,11... | collective-permute-start | bytes 294920 | tf_op jit(solution)/shard_map/ppermute | solution.py:238
  30.6 6.6 %collective-permute-start.1 = (bf16[1,3,16,1024]{3,2,1,0:T(8,128)(2,1)S(1)}, bf16[1,3,16,1024]{3,2,1,0:T(8,128)(2,1)S(1)}, u32[]{:S(2)}, u32[]{:S(2)}) collective-permute-start(bf16[1,3,16,1024]{3,2,1,0:T(8,128)(2,1)S(1)} %shard_map.49.refs_0_), channel_id=1, source_target_pairs={{0,64},{32,96},{64,128},{96,160},{128,192},{160,224},{192,0},{224,... | collective-permute-start | bytes 294920 | tf_op jit(solution)/shard_map/ppermute | solution.py:242
  33.1 11.6 %collective-permute-start.6 = (bf16[3,3,16,1024]{3,2,1,0:T(8,128)(2,1)S(1)}, bf16[3,3,16,1024]{3,2,1,0:T(8,128)(2,1)S(1)}, u32[]{:S(2)}, u32[]{:S(2)}) collective-permute-start(bf16[3,3,16,1024]{3,2,1,0:T(8,128)(2,1)S(1)} %shard_map.52), channel_id=1, source_target_pairs={{0,224},{32,0},{64,32},{96,64},{128,96},{160,128},{192,160},{224,1... | collective-permute-start | bytes 884744 | tf_op jit(solution)/shard_map/ppermute | solution.py:242
  37.3 7.4 %collective-permute-start.5 = (bf16[3,3,16,1024]{3,2,1,0:T(8,128)(2,1)S(1)}, bf16[3,3,16,1024]{3,2,1,0:T(8,128)(2,1)S(1)}, u32[]{:S(2)}, u32[]{:S(2)}) collective-permute-start(bf16[3,3,16,1024]{3,2,1,0:T(8,128)(2,1)S(1)} %shard_map.51), channel_id=1, source_target_pairs={{0,32},{32,64},{64,96},{96,128},{128,160},{160,192},{192,224},{224... | collective-permute-start | bytes 884744 | tf_op jit(solution)/shard_map/ppermute | solution.py:242
  37.4 7.3 %collective-permute-start.4 = (bf16[2,3,16,1024]{3,2,1,0:T(8,128)(2,1)S(1)}, bf16[2,3,16,1024]{3,2,1,0:T(8,128)(2,1)S(1)}, u32[]{:S(2)}, u32[]{:S(2)}) collective-permute-start(bf16[2,3,16,1024]{3,2,1,0:T(8,128)(2,1)S(1)} %shard_map.50.after_ref), channel_id=1, source_target_pairs={{0,1},{1,0},{2,3},{3,2},{4,5},{5,4},{6,7},{7,6},{8,9},{9,8},{10,11... | collective-permute-start | bytes 589832 | tf_op jit(solution)/shard_map/ppermute | solution.py:238
  37.6 5.2 %collective-permute-start.7 = (bf16[1,3,16,512]{3,2,1,0:T(8,128)(2,1)S(1)}, bf16[1,3,16,512]{3,2,1,0:T(8,128)(2,1)S(1)}, u32[]{:S(2)}, u32[]{:S(2)}) collective-permute-start(bf16[1,3,16,512]{3,2,1,0:T(8,128)(2,1)S(1)} %get-tuple-element.45), channel_id=1, source_target_pairs={{0,192},{32,224},{64,0},{96,32},{128,64},{160,96},{192,128},{224,1... | collective-permute-start | bytes 147464 | tf_op jit(solution)/shard_map/ppermute | solution.py:242
  39.2 5.5 %collective-permute-start.8 = (bf16[1,3,16,512]{3,2,1,0:T(8,128)(2,1)S(1)}, bf16[1,3,16,512]{3,2,1,0:T(8,128)(2,1)S(1)}, u32[]{:S(2)}, u32[]{:S(2)}) collective-permute-start(bf16[1,3,16,512]{3,2,1,0:T(8,128)(2,1)S(1)} %get-tuple-element.46), channel_id=1, source_target_pairs={{0,64},{32,96},{64,128},{96,160},{128,192},{160,224},{192,0},{224,... | collective-permute-start | bytes 147464 | tf_op jit(solution)/shard_map/ppermute | solution.py:242
  44.8 9.3 %collective-permute-start.9 = (bf16[13,3,16,1024]{3,2,1,0:T(8,128)(2,1)S(1)}, bf16[13,3,16,1024]{3,2,1,0:T(8,128)(2,1)S(1)}, u32[]{:S(2)}, u32[]{:S(2)}) collective-permute-start(bf16[13,3,16,1024]{3,2,1,0:T(8,128)(2,1)S(1)} %shard_map.56.middle), channel_id=1, source_target_pairs={{0,16},{16,0},{1,17},{17,1},{2,18},{18,2},{3,19},{19,3},{4,20},{20... | collective-permute-start | bytes 3833864 | tf_op jit(solution)/shard_map/ppermute | solution.py:238
  50.1 9.1 %collective-permute-start.10 = (bf16[1,3,16,1024]{3,2,1,0:T(8,128)(2,1)S(1)}, bf16[1,3,16,1024]{3,2,1,0:T(8,128)(2,1)S(1)}, u32[]{:S(2)}, u32[]{:S(2)}) collective-permute-start(bf16[1,3,16,1024]{3,2,1,0:T(8,128)(2,1)S(1)} %shard_map.55.refs_7_), channel_id=1, source_target_pairs={{0,1},{1,0},{2,3},{3,2},{4,5},{5,4},{6,7},{7,6},{8,9},{9,8},{10,11... | collective-permute-start | bytes 294920 | tf_op jit(solution)/shard_map/ppermute | solution.py:238
  51.5 5.3 %collective-permute-start.12 = (bf16[1,3,16,1024]{3,2,1,0:T(8,128)(2,1)S(1)}, bf16[1,3,16,1024]{3,2,1,0:T(8,128)(2,1)S(1)}, u32[]{:S(2)}, u32[]{:S(2)}) collective-permute-start(bf16[1,3,16,1024]{3,2,1,0:T(8,128)(2,1)S(1)} %get-tuple-element.53), channel_id=1, source_target_pairs={{0,32},{32,64},{64,96},{96,128},{128,160},{160,192},{192,224},{224... | collective-permute-start | bytes 294920 | tf_op jit(solution)/shard_map/ppermute | solution.py:242
  53.9 3.8 %collective-permute-start.13 = (bf16[1,3,16,1024]{3,2,1,0:T(8,128)(2,1)S(1)}, bf16[1,3,16,1024]{3,2,1,0:T(8,128)(2,1)S(1)}, u32[]{:S(2)}, u32[]{:S(2)}) collective-permute-start(bf16[1,3,16,1024]{3,2,1,0:T(8,128)(2,1)S(1)} %get-tuple-element.54), channel_id=1, source_target_pairs={{0,224},{32,0},{64,32},{96,64},{128,96},{160,128},{192,160},{224,1... | collective-permute-start | bytes 294920 | tf_op jit(solution)/shard_map/ppermute | solution.py:242
  57.6 2.8 %collective-permute-start.14 = (bf16[2,3,16,1024]{3,2,1,0:T(8,128)(2,1)S(1)}, bf16[2,3,16,1024]{3,2,1,0:T(8,128)(2,1)S(1)}, u32[]{:S(2)}, u32[]{:S(2)}) collective-permute-start(bf16[2,3,16,1024]{3,2,1,0:T(8,128)(2,1)S(1)} %shard_map.59.last), channel_id=1, source_target_pairs={{0,16},{16,0},{1,17},{17,1},{2,18},{18,2},{3,19},{19,3},{4,20},{20... | collective-permute-start | bytes 589832 | tf_op jit(solution)/shard_map/ppermute | solution.py:238
  59.2 1.3 %collective-permute-start.11 = (bf16[1,3,16,1024]{3,2,1,0:T(8,128)(2,1)S(1)}, bf16[1,3,16,1024]{3,2,1,0:T(8,128)(2,1)S(1)}, u32[]{:S(2)}, u32[]{:S(2)}) collective-permute-start(bf16[1,3,16,1024]{3,2,1,0:T(8,128)(2,1)S(1)} %collective-permute-done.10.across), channel_id=1, source_target_pairs={{0,16},{16,0},{1,17},{17,1},{2,18},{18,2},{3,19},{19,3},{4,20},{20... | collective-permute-start | bytes 294920 | tf_op jit(solution)/shard_map/ppermute | solution.py:238
